TPU v7x, 32 devices: a whole 2x2x4 slice. The times are simulated.
32 devices in a mesh: batch: 8 (over z, x), head: 4 (over y, core).
Axes of the slice: x: 2, y: 2, z: 4, core: 2. Of those that a mesh axis runs over, the one named last changes fastest.
Arguments:
- tokens_in: bfloat16 [32768, 512], P(('batch', 'head')), may hold values from -6 to 6
- norm1_gain: bfloat16 [512], replicated, may hold values from 0.5 to 1.5
- norm1_bias: bfloat16 [512], replicated, may hold values from -3 to 3
- qkv_weight: bfloat16 [512, 3, 512], P(None, None, 'head'), may hold values from -0.25 to 0.25
- qkv_bias: bfloat16 [3, 512], P(None, 'head'), may hold values from -3 to 3
- out_weight: bfloat16 [512, 512], P('head'), may hold values from -1.5 to 1.5
- out_bias: bfloat16 [512], replicated, may hold values from -3 to 3
- norm2_gain: bfloat16 [512], replicated, may hold values from 0.5 to 1.5
- norm2_bias: bfloat16 [512], replicated, may hold values from -3 to 3
- up_weight: bfloat16 [512, 2048], P(None, 'head'), may hold values from -0.25 to 0.25
- up_bias: bfloat16 [2048], P('head'), may hold values from -3 to 3
- down_weight: bfloat16 [2048, 512], P('head'), may hold values from -0.125 to 0.125
- down_bias: bfloat16 [512], replicated, may hold values from -3 to 3
- cotangent: bfloat16 [32768, 512], P(('batch', 'head')), may hold values from -6 to 6
- long_slot: int32 [16], P('batch'), may hold values 0 or 1
Outputs:
- layer_out: bfloat16 [32768, 512], P(('batch', 'head'))
- input_grad: bfloat16 [32768, 512], P(('batch', 'head'))
- norm1_gain_grad: float32 [512], replicated
- norm1_bias_grad: float32 [512], replicated
- qkv_weight_grad: float32 [512, 3, 512], P(None, None, 'head')
- qkv_bias_grad: float32 [3, 512], P(None, 'head')
- out_weight_grad: float32 [512, 512], P('head')
- out_bias_grad: float32 [512], replicated
- norm2_gain_grad: float32 [512], replicated
- norm2_bias_grad: float32 [512], replicated
- up_weight_grad: float32 [512, 2048], P(None, 'head')
- up_bias_grad: float32 [2048], P('head')
- down_weight_grad: float32 [2048, 512], P('head')
- down_bias_grad: float32 [512], replicated
Inputs may be any that keep to these rules, and one draw needn't show every extreme that they name: `long_slot`: 1: the slot's 2048 tokens are one sequence; 0: they are two sequences of 1024 tokens.
All inputs are finite; a program needn't handle non-finite values. No bound on the sum of `long_slot` on one device may be relied on, other than what follows from the above.
Results may differ from a plain program's by a relative error of at most 0.017.
Values may be sent and summed in bfloat16 or wider, within the bound.
No kernel may reach another device: no remote copies, remote signals or barrier semaphores. Data moves between devices by JAX's collectives and lax.ppermute only.
A program may use at most 256 MiB of HBM per device.

v0:
```python
from functools import partial

import jax
import jax.numpy as jnp
from jax import lax
from jax.sharding import PartitionSpec as P

HD = 64
SHORT = 1024


def layer_norm(row_values, gain_vector, bias_vector):
    centered = row_values - jnp.mean(row_values, axis=-1, keepdims=True)
    variance = jnp.mean(centered * centered, axis=-1, keepdims=True)
    return centered * lax.rsqrt(variance + 1e-05) * gain_vector + bias_vector


def gelu_tanh(pre_activation):
    cubic = pre_activation + 0.044715 * pre_activation * pre_activation * pre_activation
    return 0.5 * pre_activation * (1.0 + jnp.tanh(0.7978845608028654 * cubic))


def block_scores(query_block, key_block, offset):
    scale_factor = query_block.shape[2] ** (-0.5)
    scores = (
        jnp.einsum("qhd,khd->hqk", query_block, key_block, preferred_element_type=jnp.float32)
        * scale_factor
    )
    query_pos = jnp.arange(query_block.shape[0], dtype=jnp.int32)[:, None] + offset
    key_pos = jnp.arange(key_block.shape[0], dtype=jnp.int32)[None, :]
    return (scores, (key_pos <= query_pos)[None])


def block_forward(start_key, begin, finish, queries, keys_in, values_in):
    value_block = values_in[start_key:finish]
    scores, visible = block_scores(
        queries[begin:finish], keys_in[start_key:finish], begin - start_key
    )
    magnitude = jnp.where(visible, jnp.abs(scores), -1e30)
    row_top = jnp.max(magnitude, axis=2, keepdims=True)
    powers = jnp.where(visible, jnp.exp(magnitude - row_top), 0.0)
    row_total = jnp.sum(powers, axis=2, keepdims=True)
    log_total = row_top + jnp.log(row_total)
    chance = powers / row_total
    signed = jnp.where(visible, jnp.sign(scores) * (chance - jnp.exp(-log_total)), 0.0)
    mixed_values = jnp.einsum(
        "hqk,khd->qhd", signed.astype(jnp.bfloat16), value_block, preferred_element_type=jnp.float32
    )
    return (mixed_values.astype(jnp.bfloat16), log_total)


def block_backward(start_key, begin, finish, queries, keys_in, values_in, grads_in, log_totals):
    length = keys_in.shape[0]
    query_block = queries[begin:finish]
    key_block = keys_in[start_key:finish]
    value_block = values_in[start_key:finish]
    grad_block = grads_in[begin:finish]
    log_total = log_totals[:, begin:finish]
    scores, visible = block_scores(query_block, key_block, begin - start_key)
    chance = jnp.where(visible, jnp.exp(jnp.abs(scores) - log_total), 0.0)
    signed = jnp.where(visible, jnp.sign(scores) * (chance - jnp.exp(-log_total)), 0.0)
    weight_grad = jnp.einsum(
        "qhd,khd->hqk", grad_block, value_block, preferred_element_type=jnp.float32
    )
    delta_sum = jnp.sum(weight_grad * signed, axis=2, keepdims=True)
    score_grad = (chance * (weight_grad - delta_sum * jnp.sign(scores))).astype(jnp.bfloat16)
    scale_factor = query_block.shape[2] ** (-0.5)
    query_grad = (
        jnp.einsum("hqk,khd->qhd", score_grad, key_block, preferred_element_type=jnp.float32)
        * scale_factor
    )
    key_grad = (
        jnp.einsum("hqk,qhd->khd", score_grad, query_block, preferred_element_type=jnp.float32)
        * scale_factor
    )
    value_grad = jnp.einsum(
        "hqk,qhd->khd", signed.astype(jnp.bfloat16), grad_block, preferred_element_type=jnp.float32
    )
    padding = ((start_key, length - finish), (0, 0), (0, 0))
    return (query_grad, jnp.pad(key_grad, padding), jnp.pad(value_grad, padding))


def block_list(length):
    block_rows = min(512, SHORT)
    listed = []
    for block_index in range(length // block_rows):
        begin = block_index * block_rows
        listed.append((begin, begin + block_rows, begin // SHORT * SHORT))
    return listed


def slot_attend(queries, keys_in, values_in, slot_flag):
    mixed_parts = []
    total_parts = []
    for begin, finish, short_start in block_list(queries.shape[0]):
        full_range = partial(block_forward, 0, begin, finish, queries, keys_in, values_in)
        if short_start == 0:
            mixed_values, log_total = full_range()
        else:
            own_range = partial(
                block_forward, short_start, begin, finish, queries, keys_in, values_in
            )
            mixed_values, log_total = lax.cond(slot_flag > 0, full_range, own_range)
        mixed_parts.append(mixed_values)
        total_parts.append(log_total)
    return (jnp.concatenate(mixed_parts, 0), jnp.concatenate(total_parts, 1))


def slot_backward(queries, keys_in, values_in, grads_in, log_totals, slot_flag):
    query_parts = []
    key_sum = jnp.zeros(keys_in.shape, jnp.float32)
    value_sum = jnp.zeros(values_in.shape, jnp.float32)
    for begin, finish, short_start in block_list(queries.shape[0]):
        full_range = partial(
            block_backward, 0, begin, finish, queries, keys_in, values_in, grads_in, log_totals
        )
        if short_start == 0:
            query_grad, key_grad, value_grad = full_range()
        else:
            own_range = partial(
                block_backward,
                short_start,
                begin,
                finish,
                queries,
                keys_in,
                values_in,
                grads_in,
                log_totals,
            )
            query_grad, key_grad, value_grad = lax.cond(slot_flag > 0, full_range, own_range)
        query_parts.append(query_grad)
        key_sum = key_sum + key_grad
        value_sum = value_sum + value_grad
    return jnp.stack([jnp.concatenate(query_parts, 0), key_sum, value_sum], axis=1)


def per_device(
    tokens_in,
    norm1_gain,
    norm1_bias,
    qkv_weight,
    qkv_bias,
    out_weight,
    out_bias,
    norm2_gain,
    norm2_bias,
    up_weight,
    up_bias,
    down_weight,
    down_bias,
    cotangent,
    long_slot,
):
    own_rows = tokens_in.shape[0]
    slot_count = long_slot.shape[0]
    group_rows = own_rows * lax.axis_size("head")
    length = group_rows // slot_count
    local_width = qkv_weight.shape[2]
    heads_here = local_width // HD
    input_rows = tokens_in.astype(jnp.float32)
    first_gain = norm1_gain.astype(jnp.float32)
    first_bias = norm1_bias.astype(jnp.float32)
    second_gain = norm2_gain.astype(jnp.float32)
    second_bias = norm2_bias.astype(jnp.float32)
    normed1 = layer_norm(input_rows, first_gain, first_bias).astype(jnp.bfloat16)
    gathered1 = lax.all_gather(normed1, "head", axis=0, tiled=True)
    triple = jnp.einsum("td,dch->tch", gathered1, qkv_weight, preferred_element_type=jnp.float32)
    triple = (triple + qkv_bias.astype(jnp.float32)).astype(jnp.bfloat16)
    split_heads = triple.reshape(slot_count, length, 3, heads_here, HD)
    attended_parts = []
    total_list = []
    for slot_index in range(slot_count):
        mixed_values, log_totals = slot_attend(
            split_heads[slot_index, :, 0],
            split_heads[slot_index, :, 1],
            split_heads[slot_index, :, 2],
            long_slot[slot_index],
        )
        attended_parts.append(mixed_values)
        total_list.append(log_totals)
    attended = jnp.concatenate(attended_parts, 0).reshape(group_rows, local_width)
    picked = attended
    branch = lax.psum_scatter(
        jnp.dot(picked, out_weight, preferred_element_type=jnp.float32),
        "head",
        scatter_dimension=0,
        tiled=True,
    )
    middle = input_rows + branch + out_bias.astype(jnp.float32)
    normed2 = layer_norm(middle, second_gain, second_bias).astype(jnp.bfloat16)
    cot_rows_f = cotangent.astype(jnp.float32)
    gathered2 = lax.all_gather(normed2, "head", axis=0, tiled=True)
    pre_activation = jnp.dot(
        gathered2, up_weight, preferred_element_type=jnp.float32
    ) + up_bias.astype(jnp.float32)
    activated = gelu_tanh(pre_activation).astype(jnp.bfloat16)
    picked = activated
    feed_out = lax.psum_scatter(
        jnp.dot(picked, down_weight, preferred_element_type=jnp.float32).astype(jnp.bfloat16),
        "head",
        scatter_dimension=0,
        tiled=True,
    ).astype(jnp.float32)
    layer_out = (middle + feed_out + down_bias.astype(jnp.float32)).astype(jnp.bfloat16)
    gathered_cot = lax.all_gather(cotangent, "head", axis=0, tiled=True)
    act_grad = jnp.einsum(
        "td,fd->tf", gathered_cot, down_weight, preferred_element_type=jnp.float32
    )
    down_grad = jnp.einsum("tf,td->fd", activated, gathered_cot, preferred_element_type=jnp.float32)
    gelu_value, gelu_pull = jax.vjp(gelu_tanh, pre_activation)
    pre_grad = gelu_pull(act_grad)[0].astype(jnp.bfloat16)
    up_grad = jnp.einsum("td,tf->df", gathered2, pre_grad, preferred_element_type=jnp.float32)
    up_bias_grad = jnp.sum(pre_grad.astype(jnp.float32), axis=0)
    picked = pre_grad
    normed2_grad = lax.psum_scatter(
        jnp.einsum("tf,df->td", picked, up_weight, preferred_element_type=jnp.float32),
        "head",
        scatter_dimension=0,
        tiled=True,
    )
    norm_value, second_pull = jax.vjp(layer_norm, middle, second_gain, second_bias)
    middle_back, second_gain_grad, second_bias_grad = second_pull(normed2_grad)
    middle_grad = cot_rows_f + middle_back
    down_bias_local = jnp.sum(cot_rows_f, axis=0)
    branch_grad = middle_grad.astype(jnp.bfloat16)
    out_bias_local = jnp.sum(branch_grad.astype(jnp.float32), axis=0)
    gathered_branch = lax.all_gather(branch_grad, "head", axis=0, tiled=True)
    attended_grad = jnp.einsum(
        "td,hd->th", gathered_branch, out_weight, preferred_element_type=jnp.float32
    ).astype(jnp.bfloat16)
    out_grad = jnp.einsum(
        "th,td->hd", attended, gathered_branch, preferred_element_type=jnp.float32
    )
    split_grads = attended_grad.reshape(slot_count, length, heads_here, HD)
    triple_parts = []
    for slot_index in range(slot_count):
        triple_parts.append(
            slot_backward(
                split_heads[slot_index, :, 0],
                split_heads[slot_index, :, 1],
                split_heads[slot_index, :, 2],
                split_grads[slot_index],
                total_list[slot_index],
                long_slot[slot_index],
            )
        )
    triple_grad = (
        jnp.concatenate(triple_parts, 0).reshape(group_rows, 3, local_width).astype(jnp.bfloat16)
    )
    qkv_grad = jnp.einsum("td,tch->dch", gathered1, triple_grad, preferred_element_type=jnp.float32)
    qkv_bias_grad = jnp.sum(triple_grad.astype(jnp.float32), axis=0)
    picked = triple_grad
    normed1_grad = lax.psum_scatter(
        jnp.einsum("tch,dch->td", picked, qkv_weight, preferred_element_type=jnp.float32),
        "head",
        scatter_dimension=0,
        tiled=True,
    )
    first_value, first_pull = jax.vjp(layer_norm, input_rows, first_gain, first_bias)
    input_back, first_gain_grad, first_bias_grad = first_pull(normed1_grad)
    input_grad = (middle_grad + input_back).astype(jnp.bfloat16)
    (
        first_gain_grad,
        first_bias_grad,
        out_bias_grad,
        second_gain_grad,
        second_bias_grad,
        down_bias_grad,
    ) = lax.psum(
        (
            first_gain_grad,
            first_bias_grad,
            out_bias_local,
            second_gain_grad,
            second_bias_grad,
            down_bias_local,
        ),
        ("batch", "head"),
    )
    qkv_grad, qkv_bias_grad, out_grad, up_grad, up_bias_grad, down_grad = (
        lax.psum(qkv_grad.astype(jnp.bfloat16), "batch").astype(jnp.float32),
        lax.psum(qkv_bias_grad.astype(jnp.bfloat16), "batch").astype(jnp.float32),
        lax.psum(out_grad.astype(jnp.bfloat16), "batch").astype(jnp.float32),
        lax.psum(up_grad.astype(jnp.bfloat16), "batch").astype(jnp.float32),
        lax.psum(up_bias_grad.astype(jnp.bfloat16), "batch").astype(jnp.float32),
        lax.psum(down_grad.astype(jnp.bfloat16), "batch").astype(jnp.float32),
    )
    return (
        layer_out,
        input_grad,
        first_gain_grad,
        first_bias_grad,
        qkv_grad,
        qkv_bias_grad,
        out_grad,
        out_bias_grad,
        second_gain_grad,
        second_bias_grad,
        up_grad,
        up_bias_grad,
        down_grad,
        down_bias_grad,
    )


def solution(mesh):
    return jax.shard_map(
        per_device,
        mesh=mesh,
        in_specs=(
            P(("batch", "head"), None),
            P(),
            P(),
            P(None, None, "head"),
            P(None, "head"),
            P("head", None),
            P(),
            P(),
            P(),
            P(None, "head"),
            P("head"),
            P("head", None),
            P(),
            P(("batch", "head"), None),
            P("batch"),
        ),
        out_specs=(
            P(("batch", "head"), None),
            P(("batch", "head"), None),
            P(),
            P(),
            P(None, None, "head"),
            P(None, "head"),
            P("head", None),
            P(),
            P(),
            P(),
            P(None, "head"),
            P("head"),
            P("head", None),
            P(),
        ),
        check_vma=False,
    )
```

profile of v0, /device:TPU:0, one launch (start us, length us, event | category | flops | bytes accessed | tf_op | source)
XLA Modules:
  0.0 1078.3 jit_solution(12425433479054144909)
XLA Ops:
  19.0 34.1 %all-gather.5.cloned.1.call-done = bf16[4096,512]{1,0:T(8,128)(2,1)} async-done(((bf16[1024,512]{1,0:T(8,128)(2,1)}), bf16[4096,512]{1,0:T(8,128)(2,1)}) %all-gather.5.cloned.1.call-update) | async-done | bytes 4194320 | tf_op jit(solution)/shard_map/all_gather | solution.py:167
  53.1 6.2 add_convert_fusion
  64.0 6.1 reshape.814
  85.2 21.8 %conditional.17 = (f32[2,512,1]{1,0,2:T(2,128)S(1)}, bf16[512,2,64]{0,2,1:T(8,128)(2,1)S(1)}) conditional(s32[]{:T(128)} %bitcast.65, (bf16[2048,2,64]{0,2,1:T(8,128)(2,1)}, bf16[2048,2,64]{0,2,1:T(8,128)(2,1)S(1)}, bf16[2048,2,64]{0,2,1:T(8,128)(2,1)}) %tuple.112, (bf16[2048,2,64]{0,2,1:T(8,128)(2,1)}, bf16[2048,2,64]{0,2,1:T(8,128)(2,1)S(1)}, ...), branch_computations={%region_12.15_spmd, %region_15.18_spmd} | conditional | flops 582025728 | bytes 30715920
  100.0 7.0 fusion.41
  107.6 12.0 %conditional.16 = (f32[2,512,1]{1,0,2:T(2,128)S(1)}, bf16[512,2,64]{0,2,1:T(8,128)(2,1)S(1)}) conditional(s32[]{:T(128)} %bitcast.65, (bf16[2048,2,64]{0,2,1:T(8,128)(2,1)}, bf16[2048,2,64]{0,2,1:T(8,128)(2,1)S(1)}, bf16[2048,2,64]{0,2,1:T(8,128)(2,1)}) %tuple.112, (bf16[2048,2,64]{0,2,1:T(8,128)(2,1)}, bf16[2048,2,64]{0,2,1:T(8,128)(2,1)S(1)}, ...), branch_computations={%region_6.9_spmd, %region_9.12_spmd} | conditional | flops 436535808 | bytes 23113744
  113.5 6.0 fusion.15
  121.0 22.0 %conditional.19 = (f32[2,512,1]{1,0,2:T(2,128)S(1)}, bf16[512,2,64]{0,2,1:T(8,128)(2,1)S(1)}) conditional(s32[]{:T(128)} %bitcast.74, (bf16[2048,2,64]{0,2,1:T(8,128)(2,1)}, bf16[2048,2,64]{0,2,1:T(8,128)(2,1)S(1)}, bf16[2048,2,64]{0,2,1:T(8,128)(2,1)}) %tuple.113, (bf16[2048,2,64]{0,2,1:T(8,128)(2,1)}, bf16[2048,2,64]{0,2,1:T(8,128)(2,1)S(1)}, ...), branch_computations={%region_28.31_spmd, %region_31.34_spmd} | conditional | flops 582025728 | bytes 30715920
  136.0 7.0 fusion.89
  143.6 12.1 %conditional.18 = (f32[2,512,1]{1,0,2:T(2,128)S(1)}, bf16[512,2,64]{0,2,1:T(8,128)(2,1)S(1)}) conditional(s32[]{:T(128)} %bitcast.74, (bf16[2048,2,64]{0,2,1:T(8,128)(2,1)}, bf16[2048,2,64]{0,2,1:T(8,128)(2,1)S(1)}, bf16[2048,2,64]{0,2,1:T(8,128)(2,1)}) %tuple.113, (bf16[2048,2,64]{0,2,1:T(8,128)(2,1)}, bf16[2048,2,64]{0,2,1:T(8,128)(2,1)S(1)}, ...), branch_computations={%region_22.25_spmd, %region_25.28_spmd} | conditional | flops 436535808 | bytes 23113744
  149.7 6.0 fusion.63
  184.1 70.6 %reduce-scatter.5.cloned.1.call-done = f32[1024,512]{1,0:T(8,128)} async-done(((f32[4096,512]{1,0:T(8,128)}), f32[1024,512]{1,0:T(8,128)}) %reduce-scatter.5.cloned.1.call-update) | async-done | bytes 2097168 | tf_op jit(solution)/shard_map/reduce_scatter | solution.py:184
  260.6 32.8 %all-gather.7.cloned.1.call-done = bf16[4096,512]{1,0:T(8,128)(2,1)} async-done(((bf16[1024,512]{1,0:T(8,128)(2,1)}), bf16[4096,512]{1,0:T(8,128)(2,1)}) %all-gather.7.cloned.1.call-update) | async-done | bytes 4194320 | tf_op jit(solution)/shard_map/all_gather | solution.py:193
  293.4 7.9 fusion.635
  301.2 28.1 %all-gather.9.cloned.1.call-done = bf16[4096,512]{1,0:T(8,128)(2,1)} async-done(((bf16[1024,512]{1,0:T(8,128)(2,1)}), bf16[4096,512]{1,0:T(8,128)(2,1)}) %all-gather.9.cloned.1.call-update) | async-done | bytes 4194320 | tf_op jit(solution)/shard_map/all_gather | solution.py:206
  329.4 12.8 %fusion.621 = (bf16[512]{0:T(512)(128)(2,1)}, bf16[4096,512]{1,0:T(8,128)(2,1)S(1)}) fusion(f32[4096,512]{1,0:T(8,128)} %fusion.635, f32[512]{0:T(512)} %convert_element_type.380, bf16[4096,512]{1,0:T(8,128)(2,1)} %all-gather.9.cloned.1.call-done, bf16[512,512]{1,0:T(8,128)(2,1)S(1)} %copy-done), kind=kOutput, calls=%fused_computation.650 | convolution fusion | flops 2202009088 | bytes 17304576 | tf_op jit(solution)/shard_map/td,fd->tf/dot_general | solution.py:207
  349.8 9.3 convolution_convert_fusion.2
  359.8 61.9 %reduce-scatter.9.cloned.1.call-done = f32[1024,512]{1,0:T(8,128)} async-done(((f32[4096,512]{1,0:T(8,128)}), f32[1024,512]{1,0:T(8,128)}) %reduce-scatter.9.cloned.1.call-update) | async-done | bytes 2097168 | tf_op jit(solution)/shard_map/reduce_scatter | solution.py:216
  424.6 44.0 %reduce-scatter.7.cloned.1.call-done = bf16[1024,512]{1,0:T(8,128)(2,1)} async-done(((bf16[4096,512]{1,0:T(8,128)(2,1)}), bf16[1024,512]{1,0:T(8,128)(2,1)}) %reduce-scatter.7.cloned.1.call-update) | async-done | bytes 1048592 | tf_op jit(solution)/shard_map/reduce_scatter | solution.py:199
  475.5 6.7 convolution_convert_fusion.5
  482.3 8.8 convolution_convert_fusion.4
  491.1 18.8 %all-gather.11.cloned.1.call-done = bf16[4096,512]{1,0:T(8,128)(2,1)} async-done(((bf16[1024,512]{1,0:T(8,128)(2,1)}), bf16[4096,512]{1,0:T(8,128)(2,1)}) %all-gather.11.cloned.1.call-update) | async-done | bytes 4194320 | tf_op jit(solution)/shard_map/all_gather | solution.py:228
  524.3 7.5 fusion.509
  557.8 11.2 %fusion.522 = bf16[512,2,64]{0,2,1:T(8,128)(2,1)} fusion(f32[2,512,1024]{2,1,0:T(8,128)} %fusion.555, f32[2,512,1024]{2,1,0:T(8,128)} %copy-done.7, f32[2,512]{1,0:T(2,128)S(1)} %copy-done.108, pred[512,1024]{1,0:T(8,128)(4,1)S(1)} %copy-done.28, f32[2,512]{1,0:T(2,128)S(1)} %copy-done.107, bf16[1,1024,1,2,64]{1,0,4,3,2:T(2,128)(2,1)S(1)} %copy-done.40), kind=kOutput, calls=%fused_computation.530 | convolution fusion | flops 153225216 | bytes 9314304 | tf_op jit(solution)/shard_map/hqk,khd->qhd/dot_general | solution.py:69
  569.0 11.6 %fusion.506 = f32[1024,2,64]{0,2,1:T(8,128)} fusion(f32[2,512,1024]{2,1,0:T(8,128)} %fusion.555, f32[2,512,1024]{2,1,0:T(8,128)} %copy-done.7, f32[2,512]{1,0:T(2,128)S(1)} %copy-done.108, pred[512,1024]{1,0:T(8,128)(4,1)S(1)} %copy-done.28, f32[2,512]{1,0:T(2,128)S(1)} %copy-done.107, bf16[1,512,1,2,64]{1,0,4,3,2:T(2,128)(2,1)S(1)} %copy-done.46), kind=kOutput, calls=%fused_computation.516 | convolution fusion | flops 153225216 | bytes 9576448 | tf_op jit(solution)/shard_map/hqk,qhd->khd/dot_general | solution.py:73
  587.9 10.8 fusion.516
  598.7 11.6 %fusion.500 = f32[1024,2,64]{0,2,1:T(8,128)} fusion(f32[2,512,1024]{2,1,0:T(8,128)} %fusion.557, f32[2,512,1024]{2,1,0:T(8,128)} %copy-done.21, f32[2,512]{1,0:T(2,128)S(1)} %copy-done.102, pred[512,1024]{1,0:T(8,128)(4,1)S(1)} %copy-done.28, f32[2,512]{1,0:T(2,128)S(1)} %copy-done.101, bf16[1,512,1,2,64]{1,0,4,3,2:T(2,128)(2,1)S(1)} %copy-done.64), kind=kOutput, calls=%fused_computation.514 | convolution fusion | flops 153225216 | bytes 9576448 | tf_op jit(solution)/shard_map/hqk,qhd->khd/dot_general | solution.py:73
  611.0 48.0 %conditional.40 = (bf16[512,2,64]{0,2,1:T(8,128)(2,1)}, f32[2048,2,64]{0,2,1:T(8,128)S(1)}, f32[2048,2,64]{0,2,1:T(8,128)S(1)}) conditional(s32[]{:T(128)} %bitcast.65, (bf16[2048,2,64]{0,2,1:T(8,128)(2,1)}, bf16[2048,2,64]{0,2,1:T(8,128)(2,1)S(1)}, f32[2,512,1]{1,0,2:T(2,128)S(1)}, bf16[2048,2,64]{0,2,1:T(8,128)(2,1)}, ...), branch_computations={%region_43.45_spmd, %region_45.47_spmd} | conditional | flops 1078532608 | bytes 84193336 | solution.py:131
  621.1 14.2 %fusion.148 = bf16[512,2,64]{0,2,1:T(8,128)(2,1)} fusion(f32[2,512,1536]{2,1,0:T(8,128)} %fusion.151, f32[2,512,1536]{2,1,0:T(8,128)} %fusion.154, f32[2,512]{1,0:T(2,128)S(1)} %bitcast.319, pred[512,1536]{1,0:T(8,128)(4,1)S(1)} %iota_compare_fusion.9, f32[2,512]{1,0:T(2,128)S(1)} %exponential_bitcast_fusion.1, bf16[2048,2,64]{0,2,1:T(8,128)(2,1)S(1)} %get-tuple-element.190), kind=kOutput, calls=%fused_computation.199 | convolution fusion | flops 229771776 | bytes 27275264 | tf_op jit(solution)/shard_map/cond/branch_1_fun/hqk,khd->qhd/dot_general | solution.py:69
  635.3 15.5 %fusion.136 = f32[1536,2,64]{0,2,1:T(8,128)} fusion(f32[2,512,1536]{2,1,0:T(8,128)} %fusion.151, f32[2,512,1536]{2,1,0:T(8,128)} %fusion.154, f32[2,512]{1,0:T(2,128)S(1)} %bitcast.320, pred[512,1536]{1,0:T(8,128)(4,1)S(1)} %iota_compare_fusion.9, f32[2,512]{1,0:T(2,128)S(1)} %exponential_bitcast_fusion.1, bf16[2048,2,64]{0,2,1:T(8,128)(2,1)} %get-tuple-element.189), kind=kOutput, calls=%fused_computation.195 | convolution fusion | flops 229837312 | bytes 27668480 | tf_op jit(solution)/shard_map/cond/branch_1_fun/hqk,qhd->khd/dot_general | solution.py:73
  650.8 7.2 fusion.137
  660.5 61.9 %conditional.41 = (bf16[512,2,64]{0,2,1:T(8,128)(2,1)S(1)}, f32[2048,2,64]{0,2,1:T(8,128)}, f32[2048,2,64]{0,2,1:T(8,128)S(1)}) conditional(s32[]{:T(128)} %bitcast.65, (bf16[2048,2,64]{0,2,1:T(8,128)(2,1)}, bf16[2048,2,64]{0,2,1:T(8,128)(2,1)S(1)}, f32[2,512,1]{1,0,2:T(2,128)S(1)}, bf16[2048,2,64]{0,2,1:T(8,128)(2,1)}, ...), branch_computations={%region_47.49_spmd, %region_49.51_spmd} | conditional | flops 2243304960 | bytes 65056820 | solution.py:131
  672.4 20.3 %fusion.228 = bf16[512,2,64]{0,2,1:T(8,128)(2,1)S(1)} fusion(bf16[2048,2,64]{0,2,1:T(8,128)(2,1)S(1)} %get-tuple-element.200, f32[2,512,2048]{2,1,0:T(8,128)} %fusion.230, f32[2,512]{1,0:T(2,128)S(1)} %bitcast.313, pred[512,2048]{1,0:T(8,128)(4,1)} %iota_compare_fusion.11, bf16[2048,2,64]{0,2,1:T(8,128)(2,1)} %get-tuple-element.203, ...), kind=kOutput, calls=%fused_computation.264 | convolution fusion | flops 843189248 | bytes 20852736 | tf_op jit(solution)/shard_map/cond/branch_1_fun/hqk,khd->qhd/dot_general | solution.py:69
  692.7 20.9 %fusion.227 = f32[2048,2,64]{0,2,1:T(8,128)} fusion(bf16[2048,2,64]{0,2,1:T(8,128)(2,1)} %get-tuple-element.199, f32[2,512,2048]{2,1,0:T(8,128)} %fusion.230, f32[2,512]{1,0:T(2,128)S(1)} %bitcast.314, pred[512,2048]{1,0:T(8,128)(4,1)} %iota_compare_fusion.11, bf16[2048,2,64]{0,2,1:T(8,128)(2,1)} %get-tuple-element.203, ...), kind=kOutput, calls=%fused_computation.262 | convolution fusion | flops 843320320 | bytes 21377024 | tf_op jit(solution)/shard_map/cond/branch_1_fun/hqk,qhd->khd/dot_general | solution.py:73
  713.6 8.5 fusion.224
  723.4 55.9 %conditional.42 = (bf16[512,2,64]{0,2,1:T(8,128)(2,1)}, f32[2048,2,64]{0,2,1:T(8,128)S(1)}, f32[2048,2,64]{0,2,1:T(8,128)S(1)}) conditional(s32[]{:T(128)} %bitcast.74, (bf16[2048,2,64]{0,2,1:T(8,128)(2,1)}, bf16[2048,2,64]{0,2,1:T(8,128)(2,1)S(1)}, f32[2,512,1]{1,0,2:T(2,128)S(1)}, bf16[2048,2,64]{0,2,1:T(8,128)(2,1)}, ...), branch_computations={%region_53.55_spmd, %region_55.57_spmd} | conditional | flops 1078532608 | bytes 86290520 | solution.py:131
  742.4 14.2 %fusion.313 = bf16[512,2,64]{0,2,1:T(8,128)(2,1)} fusion(f32[2,512,1536]{2,1,0:T(8,128)} %fusion.316, f32[2,512,1536]{2,1,0:T(8,128)} %fusion.319, f32[2,512]{1,0:T(2,128)S(1)} %bitcast.331, pred[512,1536]{1,0:T(8,128)(4,1)S(1)} %iota_compare_fusion.13, f32[2,512]{1,0:T(2,128)S(1)} %exponential_bitcast_fusion.5, ...), kind=kOutput, calls=%fused_computation.324 | convolution fusion | flops 229771776 | bytes 27275264 | tf_op jit(solution)/shard_map/cond/branch_1_fun/hqk,khd->qhd/dot_general | solution.py:69
  756.6 15.1 %fusion.301 = f32[1536,2,64]{0,2,1:T(8,128)} fusion(f32[2,512,1536]{2,1,0:T(8,128)} %fusion.316, f32[2,512,1536]{2,1,0:T(8,128)} %fusion.319, f32[2,512]{1,0:T(2,128)S(1)} %bitcast.332, pred[512,1536]{1,0:T(8,128)(4,1)S(1)} %iota_compare_fusion.13, f32[2,512]{1,0:T(2,128)S(1)} %exponential_bitcast_fusion.5, bf16[2048,2,64]{0,2,1:T(8,128)(2,1)S(1)} %copy-done.32), kind=kOutput, calls=%fused_computation.320 | convolution fusion | flops 229837312 | bytes 27668480 | tf_op jit(solution)/shard_map/cond/branch_1_fun/hqk,qhd->khd/dot_general | solution.py:73
  771.7 7.2 fusion.302
  780.3 63.7 %conditional.43 = (bf16[512,2,64]{0,2,1:T(8,128)(2,1)}, f32[2048,2,64]{0,2,1:T(8,128)}, f32[2048,2,64]{0,2,1:T(8,128)}) conditional(s32[]{:T(128)} %bitcast.74, (bf16[2048,2,64]{0,2,1:T(8,128)(2,1)}, bf16[2048,2,64]{0,2,1:T(8,128)(2,1)S(1)}, f32[2,512,1]{1,0,2:T(2,128)S(1)}, bf16[2048,2,64]{0,2,1:T(8,128)(2,1)}, ...), branch_computations={%region_57.59_spmd, %region_59.61_spmd} | conditional | flops 2243304960 | bytes 65056820 | solution.py:131
  792.9 20.8 %fusion.393 = bf16[512,2,64]{0,2,1:T(8,128)(2,1)} fusion(bf16[2048,2,64]{0,2,1:T(8,128)(2,1)S(1)} %get-tuple-element.220, f32[2,512,2048]{2,1,0:T(8,128)} %fusion.395, f32[2,512]{1,0:T(2,128)S(1)} %bitcast.325, pred[512,2048]{1,0:T(8,128)(4,1)} %iota_compare_fusion.15, bf16[2048,2,64]{0,2,1:T(8,128)(2,1)} %get-tuple-element.223, ...), kind=kOutput, calls=%fused_computation.389 | convolution fusion | flops 843189248 | bytes 20852736 | tf_op jit(solution)/shard_map/cond/branch_1_fun/hqk,khd->qhd/dot_general | solution.py:69
  813.8 20.9 %fusion.392 = f32[2048,2,64]{0,2,1:T(8,128)} fusion(bf16[2048,2,64]{0,2,1:T(8,128)(2,1)} %get-tuple-element.219, f32[2,512,2048]{2,1,0:T(8,128)} %fusion.395, f32[2,512]{1,0:T(2,128)S(1)} %bitcast.326, pred[512,2048]{1,0:T(8,128)(4,1)} %iota_compare_fusion.15, bf16[2048,2,64]{0,2,1:T(8,128)(2,1)} %get-tuple-element.223, ...), kind=kOutput, calls=%fused_computation.387 | convolution fusion | flops 843320320 | bytes 21377024 | tf_op jit(solution)/shard_map/cond/branch_1_fun/hqk,qhd->khd/dot_general | solution.py:73
  834.7 9.1 fusion.389
  860.6 7.5 convolution_bitcast_fusion.2
  868.8 21.9 %all-reduce.21 = (bf16[3,128]{1,0:T(4,128)(2,1)S(1)}, bf16[512]{0:T(512)(128)(2,1)S(1)}) all-reduce(bf16[3,128]{1,0:T(4,128)(2,1)S(1)} %reduce_sum.435, bf16[512]{0:T(512)(128)(2,1)S(1)} %copy-done.119), channel_id=1, replica_groups=mesh['batch'=8,'head'=4] {'batch'}, use_global_device_ids=true, to_apply=%region_70.71 | all-reduce | flops 896 | bytes 3584 | tf_op jit(solution)/shard_map/psum | solution.py:283
  891.9 59.2 %all-reduce.25.cloned.1.call-done = (bf16[512,3,128]{2,0,1:T(8,128)(2,1)}, bf16[128,512]{1,0:T(8,128)(2,1)}, bf16[512,512]{1,0:T(8,128)(2,1)}, bf16[512,512]{1,0:T(8,128)(2,1)}) async-done(((bf16[512,3,128]{2,0,1:T(8,128)(2,1)}, bf16[128,512]{1,0:T(8,128)(2,1)}, bf16[512,512]{1,0:T(8,128)(2,1)}, bf16[512,512]{1,0:T(8,128)(2,1)}), (bf16[512,3,128]{2,0,1:T(8,128)(2,1)}, bf16[128,512]{1,0:T(8,128)(2,1)}, ...) | async-done | bytes 1572880 | tf_op jit(solution)/shard_map/psum | solution.py:282
  959.0 66.0 %reduce-scatter.11.cloned.1.call-done = f32[1024,512]{1,0:T(8,128)} async-done(((f32[4096,512]{1,0:T(8,128)}), f32[1024,512]{1,0:T(8,128)}) %reduce-scatter.11.cloned.1.call-update) | async-done | bytes 2097168 | tf_op jit(solution)/shard_map/reduce_scatter | solution.py:254
  1032.0 39.5 %all-reduce.20 = (f32[512]{0:T(512)}, f32[512]{0:T(512)}, f32[512]{0:T(512)}, f32[512]{0:T(512)}, f32[512]{0:T(512)}, /*index=5*/f32[512]{0:T(512)}) all-reduce(f32[512]{0:T(512)S(1)} %get-tuple-element.280, f32[512]{0:T(512)S(1)} %get-tuple-element.283, ...), channel_id=1, replica_groups=mesh['batch'=8,'head'=4] {'batch','head'}, use_global_device_ids=true, to_apply=%region_65.66 | all-reduce | flops 3072 | bytes 24576 | tf_op jit(solution)/shard_map/psum | solution.py:270
  (387 shorter events, 227.9 us)
Async XLA Ops:
  7.2 322.2 %copy-start = (bf16[512,512]{1,0:T(8,128)(2,1)S(1)}, bf16[512,512]{1,0:T(8,128)(2,1)}, u32[]{:S(2)}) copy-start(bf16[512,512]{1,0:T(8,128)(2,1)} %param.42) | copy-start | bytes 1572868
  7.2 8.6 copy-start.113
  7.2 10.5 copy-start.114
  7.2 45.9 %copy-start.61 = (bf16[512,3,128]{2,0,1:T(8,128)(2,1)S(1)}, bf16[512,3,128]{2,0,1:T(8,128)(2,1)}, u32[]{:S(2)}) copy-start(bf16[512,3,128]{2,0,1:T(8,128)(2,1)} %param.34) | copy-start | bytes 1179652
  7.2 45.8 %all-gather.5.cloned.1.call-start = ((), (), s32[]{:S(2)}) async-start(), calls=%async_computation.4 | async-start | bytes 5242880 | tf_op jit(solution)/shard_map/all_gather | solution.py:167
  15.7 239.0 %reduce-scatter.5.cloned.1.call-start = ((), (), s32[]{:S(2)}) async-start(), calls=%async_computation.5 | async-start | bytes 10485760 | tf_op jit(solution)/shard_map/reduce_scatter | solution.py:184
  83.6 23.4 %copy-start.16 = (bf16[2048,2,64]{0,2,1:T(8,128)(2,1)}, bf16[2048,2,64]{0,2,1:T(8,128)(2,1)S(1)}, u32[]{:S(2)}) copy-start(bf16[2048,2,64]{0,2,1:T(8,128)(2,1)S(1)} %get-tuple-element.394) | copy-start | bytes 1572868
  121.0 22.0 %copy-start.18 = (bf16[2048,2,64]{0,2,1:T(8,128)(2,1)}, bf16[2048,2,64]{0,2,1:T(8,128)(2,1)S(1)}, u32[]{:S(2)}) copy-start(bf16[2048,2,64]{0,2,1:T(8,128)(2,1)S(1)} %get-tuple-element.391) | copy-start | bytes 1572868
  143.1 12.7 %copy-start.47 = (bf16[1,512,1,2,64]{1,0,4,3,2:T(2,128)(2,1)S(1)}, bf16[1,512,1,2,64]{1,0,4,3,2:T(2,128)(2,1)}, u32[]{:S(2)}) copy-start(bf16[1,512,1,2,64]{1,0,4,3,2:T(2,128)(2,1)} %get-tuple-element.371) | copy-start | bytes 393220
  143.1 12.7 %copy-start.48 = (bf16[1,512,1,2,64]{1,0,4,3,2:T(2,128)(2,1)S(1)}, bf16[1,512,1,2,64]{1,0,4,3,2:T(2,128)(2,1)}, u32[]{:S(2)}) copy-start(bf16[1,512,1,2,64]{1,0,4,3,2:T(2,128)(2,1)} %get-tuple-element.370) | copy-start | bytes 393220
  143.1 13.2 %copy-start.65 = (bf16[1,512,1,2,64]{1,0,4,3,2:T(2,128)(2,1)S(1)}, bf16[1,512,1,2,64]{1,0,4,3,2:T(2,128)(2,1)}, u32[]{:S(2)}) copy-start(bf16[1,512,1,2,64]{1,0,4,3,2:T(2,128)(2,1)} %get-tuple-element.368) | copy-start | bytes 393220
  143.1 13.2 %copy-start.67 = (bf16[1,512,1,2,64]{1,0,4,3,2:T(2,128)(2,1)S(1)}, bf16[1,512,1,2,64]{1,0,4,3,2:T(2,128)(2,1)}, u32[]{:S(2)}) copy-start(bf16[1,512,1,2,64]{1,0,4,3,2:T(2,128)(2,1)} %get-tuple-element.367) | copy-start | bytes 393220
  157.3 14.9 %copy-start.30 = (f32[2,512,512]{1,2,0:T(8,128)}, f32[2,512,512]{1,2,0:T(8,128)S(1)}, u32[]{:S(2)}) copy-start(f32[2,512,512]{1,2,0:T(8,128)S(1)} %get-tuple-element.384) | copy-start | bytes 6291460
  159.1 13.1 %copy-start.109 = (f32[2,512]{1,0:T(2,128)}, f32[2,512]{1,0:T(2,128)S(1)}, u32[]{:S(2)}) copy-start(f32[2,512]{1,0:T(2,128)S(1)} %get-tuple-element.317) | copy-start | bytes 12292
  164.7 9.2 copy-start.21
  182.8 110.6 %all-gather.7.cloned.1.call-start = ((), (), s32[]{:S(2)}) async-start(), calls=%async_computation.6 | async-start | bytes 5242880 | tf_op jit(solution)/shard_map/all_gather | solution.py:193
  258.7 70.6 %all-gather.9.cloned.1.call-start = ((), (), s32[]{:S(2)}) async-start(), calls=%async_computation.8 | async-start | bytes 5242880 | tf_op jit(solution)/shard_map/all_gather | solution.py:206
  259.3 162.3 %reduce-scatter.9.cloned.1.call-start = ((), (), s32[]{:S(2)}) async-start(), calls=%async_computation.9 | async-start | bytes 10485760 | tf_op jit(solution)/shard_map/reduce_scatter | solution.py:216
  329.4 14.8 %copy-start.34 = (bf16[512,512]{1,0:T(8,128)(2,1)S(1)}, bf16[512,512]{1,0:T(8,128)(2,1)}, u32[]{:S(2)}) copy-start(bf16[512,512]{1,0:T(8,128)(2,1)} %param.40) | copy-start | bytes 1572868
  349.8 118.8 %reduce-scatter.7.cloned.1.call-start = ((), (), s32[]{:S(2)}) async-start(), calls=%async_computation.7 | async-start | bytes 5242880 | tf_op jit(solution)/shard_map/reduce_scatter | solution.py:199
  359.1 150.8 %all-gather.11.cloned.1.call-start = ((), (), s32[]{:S(2)}) async-start(), calls=%async_computation.10 | async-start | bytes 5242880 | tf_op jit(solution)/shard_map/all_gather | solution.py:228
  472.0 10.3 copy-start.84
  475.3 7.0 copy-start.112
  475.3 475.8 %all-reduce.25.cloned.1.call-start = ((), (), s32[]{:S(2)}) async-start(), calls=%async_computation.12 | async-start | bytes 3145728 | tf_op jit(solution)/shard_map/psum | solution.py:282
  491.1 24.4 %copy-start.53 = (bf16[1,512,1,2,64]{1,0,4,3,2:T(2,128)(2,1)S(1)}, bf16[1,512,1,2,64]{1,0,4,3,2:T(2,128)(2,1)}, u32[]{:S(2)}) copy-start(bf16[1,512,1,2,64]{1,0,4,3,2:T(2,128)(2,1)} %get-tuple-element.365) | copy-start | bytes 393220
  524.3 7.6 copy-start.51
  524.3 10.3 copy-start.13
  524.3 10.3 copy-start.104
  524.3 10.3 copy-start.105
  543.6 9.8 copy-start.107
  543.6 9.8 copy-start.108
  557.8 11.2 %copy-start.46 = (bf16[1,512,1,2,64]{1,0,4,3,2:T(2,128)(2,1)S(1)}, bf16[1,512,1,2,64]{1,0,4,3,2:T(2,128)(2,1)}, u32[]{:S(2)}) copy-start(bf16[1,512,1,2,64]{1,0,4,3,2:T(2,128)(2,1)} %get-tuple-element.369) | copy-start | bytes 393220
  569.0 11.6 %copy-start.38 = (bf16[1,1024,1,2,64]{1,0,4,3,2:T(2,128)(2,1)S(1)}, bf16[1,1024,1,2,64]{1,0,4,3,2:T(2,128)(2,1)}, u32[]{:S(2)}) copy-start(bf16[1,1024,1,2,64]{1,0,4,3,2:T(2,128)(2,1)} %get-tuple-element.361) | copy-start | bytes 786436
  587.9 10.8 copy-start.64
  598.7 11.6 %copy-start.17 = (bf16[2048,2,64]{0,2,1:T(8,128)(2,1)S(1)}, bf16[2048,2,64]{0,2,1:T(8,128)(2,1)}, u32[]{:S(2)}) copy-start(bf16[2048,2,64]{0,2,1:T(8,128)(2,1)} %copy-done.16) | copy-start | bytes 1572868
  598.7 11.6 %copy-start.91 = (f32[2,512,1]{1,0,2:T(2,128)S(1)}, f32[2,512,1]{1,0,2:T(2,128)}, u32[]{:S(2)}) copy-start(f32[2,512,1]{1,0,2:T(2,128)} %copy-done.90) | copy-start | bytes 12292
  650.8 7.3 copy-start.43
  771.7 7.3 copy-start.44
  779.3 66.5 %copy-start.69 = (f32[512,2,64]{0,2,1:T(8,128)S(1)}, f32[512,2,64]{0,2,1:T(8,128)}, u32[]{:S(2)}) copy-start(f32[512,2,64]{0,2,1:T(8,128)} %convolution_bitcast_fusion.3) | copy-start | bytes 786436
  860.6 164.5 %reduce-scatter.11.cloned.1.call-start = ((), (), s32[]{:S(2)}) async-start(), calls=%async_computation.11 | async-start | bytes 10485760 | tf_op jit(solution)/shard_map/reduce_scatter | solution.py:254
  868.2 156.9 %copy-start.3 = (bf16[1024,512]{1,0:T(8,128)(2,1)S(1)}, bf16[1024,512]{1,0:T(8,128)(2,1)}, u32[]{:S(2)}) copy-start(bf16[1024,512]{1,0:T(8,128)(2,1)} %param.31) | copy-start | bytes 3145732
  868.2 156.9 %copy-start.72 = (f32[1024]{0:T(1024)S(1)}, f32[1024]{0:T(1024)}, u32[]{:S(2)}) copy-start(f32[1024]{0:T(1024)} %copy-done.71) | copy-start | bytes 12292
  868.2 156.9 %copy-start.83 = (f32[512]{0:T(512)S(1)}, f32[512]{0:T(512)}, u32[]{:S(2)}) copy-start(f32[512]{0:T(512)} %copy-done.82) | copy-start | bytes 6148
  868.2 159.3 %copy-start.87 = (f32[1024]{0:T(1024)S(1)}, f32[1024]{0:T(1024)}, u32[]{:S(2)}) copy-start(f32[1024]{0:T(1024)} %copy-done.86) | copy-start | bytes 12292
  868.2 159.3 %copy-start.81 = (f32[1024]{0:T(1024)S(1)}, f32[1024]{0:T(1024)}, u32[]{:S(2)}) copy-start(f32[1024]{0:T(1024)} %copy-done.80) | copy-start | bytes 12292
  956.8 72.0 %copy-start.11 = (bf16[1024,512]{1,0:T(8,128)(2,1)S(1)}, bf16[1024,512]{1,0:T(8,128)(2,1)}, u32[]{:S(2)}) copy-start(bf16[1024,512]{1,0:T(8,128)(2,1)} %param.44) | copy-start | bytes 3145732
  956.8 72.0 %copy-start.85 = (f32[1024]{0:T(1024)S(1)}, f32[1024]{0:T(1024)}, u32[]{:S(2)}) copy-start(f32[1024]{0:T(1024)} %copy-done.84) | copy-start | bytes 12292
  1027.5 44.0 %copy-start.1 = (bf16[512,512]{1,0:T(8,128)(2,1)S(1)}, bf16[512,512]{1,0:T(8,128)(2,1)}, u32[]{:S(2)}) copy-start(bf16[512,512]{1,0:T(8,128)(2,1)} %param.42) | copy-start | bytes 1572868
  (81 other events, 226.2 us)
Sparse Core Ops, SparseCore 0:
  15.9 37.1 all-gather.4
  182.9 71.7 reduce-scatter.4
  258.9 34.4 all-gather.6
  294.9 34.4 all-gather.8
  349.9 71.7 reduce-scatter.8
  424.0 44.5 reduce-scatter.6
  475.4 34.4 all-gather.10
  860.7 90.3 all-reduce.24
  953.9 71.1 reduce-scatter.10
where the time goes:
time: 1090 us; the launch traced here: 1080 us
  matrix products  426 us (39%)
  waiting for transfers between devices  416 us (38%)
  other arithmetic  71.1 us (7%)
  blocking collectives  61.4 us (6%)
  local copies, waits for them, and re-layouts  47 us (4%)
  loops' own time  38.5 us (4%)
  between operations  16.7 us (2%)
    dot_general x8, matrix products, block_backward(): jnp.einsum('hqk,qhd->khd', score_grad, query_block, preferred_element_typ...  109 us
    dot_general x8, matrix products, block_backward(): jnp.einsum('hqk,khd->qhd', score_grad, key_block, preferred_element_type=...  103 us
    reduce_scatter x1, waiting for transfers between devices, per_device(): lax.psum_scatter(jnp.dot(picked, out_weight, preferred_element_type=jnp.f...  70.6 us
    reduce_scatter x1, waiting for transfers between devices, per_device(): lax.psum_scatter(jnp.einsum('tch,dch->td', picked, qkv_weight, preferred_...  66 us
    reduce_scatter x1, waiting for transfers between devices, per_device(): lax.psum_scatter(jnp.einsum('tf,df->td', picked, up_weight, preferred_ele...  61.9 us
    psum x1, waiting for transfers between devices, per_device(): lax.psum(qkv_grad.astype(jnp.bfloat16), 'batch').astype(jnp.float32)  59.2 us
    dot_general x8, matrix products, block_backward(): jnp.einsum('hqk,qhd->khd', signed.astype(jnp.bfloat16), grad_block, prefe...  45.7 us
    reduce_scatter x1, waiting for transfers between devices, per_device(): lax.psum_scatter(jnp.dot(picked, down_weight, preferred_element_type=jnp....  44 us
  transfers between devices with their start and end apart: 9, of which 9 were waited for; matrix products, arithmetic and copies ran while one was open for 5% of the time, Pallas kernels for 0%

commit v1 on v0

v1 whole, which is shorter than its diff:
```python
import functools

import jax
import jax.numpy as jnp
from jax import lax
from jax.experimental import pallas as pl
from jax.experimental.pallas import tpu as pltpu
from jax.sharding import PartitionSpec as P

HD = 64
SHORT = 1024
F32 = jnp.float32
BF = jnp.bfloat16
LOG2E = 1.4426950408889634
GELU_C = 0.7978845608028654
CHUNK = 512
VMEM_LIMIT = 56 * 1024 * 1024


def nt(a, b):
    return lax.dot_general(a, b, (((1,), (1,)), ((), ())), preferred_element_type=F32)


def nn(a, b):
    return lax.dot_general(a, b, (((1,), (0,)), ((), ())), preferred_element_type=F32)


def tn(a, b):
    return lax.dot_general(a, b, (((0,), (0,)), ((), ())), preferred_element_type=F32)


def head_mask(shape, h):
    lane = lax.broadcasted_iota(jnp.int32, shape, len(shape) - 1)
    return (lane >= h * HD) & (lane < (h + 1) * HD)


def lane_sum(e):
    width = min(128, e.shape[1])
    total = e[:, :width]
    for i in range(1, e.shape[1] // width):
        total = total + e[:, i * width : (i + 1) * width]
    return total


def fwd_kernel(bq, bk, nh, W, L, flag_ref, q_ref, k_ref, v_ref, o_ref, st_ref, *rest):
    nck = L // CHUNK
    w_refs = rest[:nck]
    kk, vm = rest[nck:]
    qi = pl.program_id(0)
    nq = L // bq

    @pl.when(qi == 0)
    def _():
        kv = k_ref[...]
        kk[...] = jnp.concatenate([kv, kv], axis=1)
        vv = v_ref[...]
        for h in range(nh):
            vm[h] = jnp.where(head_mask(vv.shape, h), vv, jnp.zeros_like(vv))

    def scaled_queries():
        qf = q_ref[...].astype(F32) * (LOG2E * HD**-0.5)
        hi = qf.astype(BF)
        lo = (qf - hi.astype(F32)).astype(BF)
        qs = []
        z = jnp.zeros_like(hi)
        for h in range(nh):
            m = head_mask(hi.shape, h)
            qs.append(jnp.concatenate([jnp.where(m, hi, z), jnp.where(m, lo, z)], axis=1))
        return qs

    def finish(acc, sums, bases):
        lane = lax.broadcasted_iota(jnp.int32, (bq, 128), 1)
        st = jnp.ones((bq, 128), F32)
        out = jnp.zeros((bq, W), F32)
        for h in range(nh):
            inv = 1.0 / sums[h]
            st = jnp.where(lane == h, inv, st)
            if bases is not None:
                st = jnp.where(lane == 8 + h, bases[h], st)
            out = jnp.where(head_mask(out.shape, h), acc * inv, out)
        st_ref[...] = st
        o_ref[...] = out.astype(BF)

    sq_r = lax.broadcasted_iota(jnp.int32, (bk, bk), 0)
    sq_c = lax.broadcasted_iota(jnp.int32, (bk, bk), 1)

    def fast(c, lo_blk):
        qs = scaled_queries()
        nr = bq // bk
        acc = [None] * nr
        ls = [[None] * nr for _ in range(nh)]
        for kb in range(lo_blk, (c + 1) * nr):
            base = kb * bk
            first = max(0, kb - c * nr)
            r0 = first * bk
            kt = kk[base : base + bk, :]
            wl = []
            for h in range(nh):
                s = nt(qs[h][r0:, :], kt)
                if base >= c * bq:
                    top = jnp.where(sq_c <= sq_r, s[:bk, :], 0.0)
                    s = top if r0 + bk == bq else jnp.concatenate([top, s[bk:, :]], axis=0)
                e = jnp.exp2(jnp.abs(s))
                wv = jnp.where(s < 0, 1.0 - e, e - 1.0).astype(BF)
                t = lane_sum(e)
                for r in range(first, nr):
                    tr = t[(r - first) * bk : (r - first + 1) * bk, :]
                    ls[h][r] = tr if ls[h][r] is None else ls[h][r] + tr
                w_refs[base // CHUNK][h, r0:, base % CHUNK : base % CHUNK + bk] = wv
                wl.append(wv)
            vcat = jnp.concatenate([vm[h, base : base + bk, :] for h in range(nh)], axis=0)
            res = nn(jnp.concatenate(wl, axis=1), vcat)
            for r in range(first, nr):
                part = res[(r - first) * bk : (r - first + 1) * bk, :]
                acc[r] = part if acc[r] is None else acc[r] + part
        row = lax.broadcasted_iota(jnp.int32, (bq, 1), 0)
        extra = (bk - 1 - row % bk).astype(F32)
        sums = [
            jnp.sum(jnp.concatenate(ls[h], axis=0), axis=1, keepdims=True) - extra
            for h in range(nh)
        ]
        finish(jnp.concatenate(acc, axis=0), sums, None)

    for c in range(nq):
        if c * bq < SHORT:
            pl.when(qi == c)(functools.partial(fast, c, 0))
        else:
            pl.when((qi == c) & (flag_ref[0] > 0))(functools.partial(fast, c, 0))
            pl.when((qi == c) & (flag_ref[0] <= 0))(functools.partial(fast, c, SHORT // bk))

    lane = lax.broadcasted_iota(jnp.int32, (bq, 128), 1)
    smallest = jnp.min(jnp.where(lane < nh, st_ref[...], 1.0))

    @pl.when(smallest < 1e-25)
    def _():
        qs = scaled_queries()
        lo_blk = jnp.where((flag_ref[0] > 0) | (qi * bq < SHORT), 0, SHORT // bk)
        hi_blk = (qi + 1) * (bq // bk)
        rows = lax.broadcasted_iota(jnp.int32, (bq, bk), 0) + qi * bq
        cols = lax.broadcasted_iota(jnp.int32, (bq, bk), 1)

        def scores(h, kb):
            kt = kk[pl.ds(pl.multiple_of(kb * bk, bk), bk), :]
            return nt(qs[h], kt), cols + kb * bk <= rows

        def top_step(kb, tops):
            new = []
            for h in range(nh):
                s, vis = scores(h, kb)
                mag = jnp.where(vis, jnp.abs(s), 0.0)
                new.append(jnp.maximum(tops[h], jnp.max(mag, axis=1, keepdims=True)))
            return tuple(new)

        tops = lax.fori_loop(lo_blk, hi_blk, top_step, (jnp.zeros((bq, 1), F32),) * nh)
        bases = [jnp.exp2(-t) for t in tops]

        def step(kb, carry):
            acc, sums = carry
            new = []
            for h in range(nh):
                s, vis = scores(h, kb)
                e = jnp.where(vis, jnp.exp2(jnp.abs(s) - tops[h]), 0.0)
                wv = jnp.where(s < 0, bases[h] - e, e - bases[h])
                wv = jnp.where(vis & (s != 0), wv, 0.0).astype(BF)
                new.append(sums[h] + jnp.sum(e, axis=1, keepdims=True))
                acc = acc + nn(wv, vm[h, pl.ds(pl.multiple_of(kb * bk, bk), bk), :])
                for j in range(nck):

                    @pl.when(kb // (CHUNK // bk) == j)
                    def _():
                        off = pl.multiple_of((kb % (CHUNK // bk)) * bk, bk)
                        w_refs[j][h, :, pl.ds(off, bk)] = wv

            return acc, tuple(new)

        acc, sums = lax.fori_loop(
            lo_blk,
            hi_blk,
            step,
            (jnp.zeros((bq, W), F32), (jnp.zeros((bq, 1), F32),) * nh),
        )
        finish(acc, sums, bases)


def w_specs(nh, bq, L):
    return [
        pl.BlockSpec((nh, bq, CHUNK), lambda qi, j=j: (0, jnp.maximum(qi, j * (CHUNK // bq)), 0))
        for j in range(L // CHUNK)
    ]


def attn_fwd(flag, q, k, v, bq=512, bk=256):
    L, W = q.shape
    nh = W // HD
    S = jax.ShapeDtypeStruct
    whole = pl.BlockSpec((L, W), lambda qi: (0, 0))
    rows = pl.BlockSpec((bq, W), lambda qi: (qi, 0))
    res = pl.pallas_call(
        functools.partial(fwd_kernel, bq, bk, nh, W, L),
        grid=(L // bq,),
        in_specs=[pl.BlockSpec(memory_space=pltpu.SMEM), rows, whole, whole],
        out_specs=[rows, pl.BlockSpec((bq, 128), lambda qi: (qi, 0))] + w_specs(nh, bq, L),
        out_shape=[S((L, W), BF), S((L, 128), F32)] + [S((nh, L, CHUNK), BF)] * (L // CHUNK),
        scratch_shapes=[pltpu.VMEM((L, 2 * W), BF), pltpu.VMEM((nh, L, W), BF)],
        compiler_params=pltpu.CompilerParams(vmem_limit_bytes=VMEM_LIMIT),
        cost_estimate=pl.CostEstimate(
            flops=8 * L * L * W, bytes_accessed=2 * nh * L * L, transcendentals=nh * L * L
        ),
        name="attn_fwd",
    )(flag, q, k, v)
    return res[0], res[1], res[2:]


def bwd_kernel(bq, bk, nh, W, L, flag_ref, q_ref, k_ref, v_ref, o_ref, do_ref, st_ref, *rest):
    nck = L // CHUNK
    w_refs = rest[:nck]
    dq_ref, dk_ref, dv_ref, km, dka, dva = rest[nck:]
    qi = pl.program_id(0)
    nq = L // bq

    @pl.when(qi == 0)
    def _():
        kv = k_ref[...]
        for h in range(nh):
            km[h] = jnp.where(head_mask(kv.shape, h), kv, jnp.zeros_like(kv))
        dka[...] = jnp.zeros_like(dka)
        dva[...] = jnp.zeros_like(dva)

    sq_r = lax.broadcasted_iota(jnp.int32, (bk, bk), 0)
    sq_c = lax.broadcasted_iota(jnp.int32, (bk, bk), 1)

    def body(c, lo_blk):
        nr = bq // bk
        tri = jnp.where(sq_c <= sq_r, 1.0, 0.0).astype(BF)
        st = st_ref[...]
        dof = do_ref[...].astype(F32)
        prod = dof * o_ref[...].astype(F32)
        dos = []
        deltas = []
        e0s = []
        dosum = jnp.zeros((bq, W), F32)
        rep = bk // 128
        for h in range(nh):
            inv = st[:, h : h + 1]
            m = head_mask((bq, W), h)
            x = jnp.where(m, dof * inv, 0.0)
            dosum = dosum + x
            dos.append(x.astype(BF))
            delta = jnp.sum(jnp.where(m, prod, 0.0), axis=1, keepdims=True) * inv
            deltas.append(jnp.concatenate([jnp.broadcast_to(delta, (bq, 128)).astype(BF)] * rep, 1))
            e0 = jnp.broadcast_to(st[:, 8 + h : 9 + h], (bq, 128)).astype(BF)
            e0s.append(jnp.concatenate([e0] * rep, 1))
        do_t = dosum.T.astype(BF)
        q_t = q_ref[...].astype(F32).T.astype(BF)
        dq = [jnp.zeros((bk, W), F32)] * nr
        for kb in range(lo_blk, (c + 1) * nr):
            base = kb * bk
            first = max(0, kb - c * nr)
            r0 = first * bk
            vt = v_ref[base : base + bk, :]
            gl = []
            for h in range(nh):
                wv = w_refs[base // CHUNK][h, r0:, base % CHUNK : base % CHUNK + bk]
                wg = nt(dos[h][r0:, :], vt).astype(BF)
                dl = deltas[h][r0:, :]
                e0 = e0s[h][r0:, :]
                if base >= c * bq:
                    top = e0[:bk, :] * tri
                    e0 = top if r0 + bk == bq else jnp.concatenate([top, e0[bk:, :]], axis=0)
                zero = jnp.zeros_like(wv)
                d = jnp.where(wv < 0, -dl, jnp.where(wv > 0, dl, zero))
                g = (jnp.abs(wv) + e0) * (wg - d)
                cols = slice(base, base + bk)
                lanes = slice(h * HD, (h + 1) * HD)
                dva[lanes, cols] += nn(do_t[lanes, r0:], wv)
                dka[lanes, cols] += nn(q_t[lanes, r0:], g)
                gl.append(g)
            kcat = jnp.concatenate([km[h, base : base + bk, :] for h in range(nh)], axis=0)
            res = nn(jnp.concatenate(gl, axis=1), kcat)
            for r in range(first, nr):
                dq[r] = dq[r] + res[(r - first) * bk : (r - first + 1) * bk, :]
        dq_ref[...] = (jnp.concatenate(dq, axis=0) * (HD**-0.5)).astype(BF)

    for c in range(nq):
        if c * bq < SHORT:
            pl.when(qi == c)(functools.partial(body, c, 0))
        else:
            pl.when((qi == c) & (flag_ref[0] > 0))(functools.partial(body, c, 0))
            pl.when((qi == c) & (flag_ref[0] <= 0))(functools.partial(body, c, SHORT // bk))

    @pl.when(qi == nq - 1)
    def _():
        dk_ref[...] = (dka[...] * (HD**-0.5)).T.astype(BF)
        dv_ref[...] = dva[...].T.astype(BF)


def attn_bwd(flag, q, k, v, o, do, st, ws, bq=512, bk=256):
    L, W = q.shape
    nh = W // HD
    whole = pl.BlockSpec((L, W), lambda qi: (0, 0))
    rows = pl.BlockSpec((bq, W), lambda qi: (qi, 0))
    return pl.pallas_call(
        functools.partial(bwd_kernel, bq, bk, nh, W, L),
        grid=(L // bq,),
        in_specs=[
            pl.BlockSpec(memory_space=pltpu.SMEM),
            rows,
            whole,
            whole,
            rows,
            rows,
            pl.BlockSpec((bq, 128), lambda qi: (qi, 0)),
        ]
        + w_specs(nh, bq, L),
        out_specs=[rows, whole, whole],
        out_shape=[jax.ShapeDtypeStruct((L, W), BF)] * 3,
        scratch_shapes=[
            pltpu.VMEM((nh, L, W), BF),
            pltpu.VMEM((W, L), F32),
            pltpu.VMEM((W, L), F32),
        ],
        compiler_params=pltpu.CompilerParams(vmem_limit_bytes=VMEM_LIMIT),
        cost_estimate=pl.CostEstimate(
            flops=16 * L * L * W, bytes_accessed=2 * nh * L * L, transcendentals=0
        ),
        name="attn_bwd",
    )(flag, q, k, v, o, do, st, *ws)


def ln_stats(v):
    c = v - jnp.mean(v, axis=1, keepdims=True)
    r = lax.rsqrt(jnp.mean(c * c, axis=1, keepdims=True) + 1e-5)
    return c * r, r


def ffn_kernel(
    nf,
    x_ref,
    att_ref,
    cot_ref,
    ow_ref,
    vec_ref,
    up_ref,
    upb_ref,
    dn_ref,
    lo_ref,
    mg_ref,
    atg_ref,
    ug_ref,
    dg_ref,
    og_ref,
    vg_ref,
    ubg_ref,
    mids,
    n2,
    n2t,
    cott,
    oacc,
    nacc,
):
    f = pl.program_id(0)

    @pl.when(f == 0)
    def _():
        mid = x_ref[...].astype(F32) + nn(att_ref[...], ow_ref[...]) + vec_ref[0:1, :]
        mids[...] = mid
        oacc[...] = mid + vec_ref[3:4, :]
        nacc[...] = jnp.zeros_like(nacc)
        xh, _ = ln_stats(mid)
        y = xh * vec_ref[1:2, :] + vec_ref[2:3, :]
        n2[...] = y.astype(BF)
        n2t[...] = y.T.astype(BF)
        cott[...] = cot_ref[...].astype(F32).T.astype(BF)

    up = up_ref[...]
    dn = dn_ref[...]
    cot = cot_ref[...]
    u = nn(n2[...], up) + upb_ref[...]
    ag = nt(cot, dn)
    u2 = u * u
    t = jnp.tanh(u * (GELU_C + (GELU_C * 0.044715) * u2))
    h = 0.5 + 0.5 * t
    act = (u * h).astype(BF)
    slope = h + u * (0.5 - 0.5 * t * t) * (GELU_C + (3 * GELU_C * 0.044715) * u2)
    pgf = ag * slope
    pg = pgf.astype(BF)
    ubg_ref[...] = jnp.sum(pgf, axis=0, keepdims=True)
    oacc[...] += nn(act, dn)
    nacc[...] += nt(pg, up)
    ug_ref[...] = nn(n2t[...], pg).astype(BF)
    dg_ref[...] = nn(cott[...], act).T.astype(BF)

    @pl.when(f == nf - 1)
    def _():
        lo_ref[...] = oacc[...].astype(BF)
        xh, r = ln_stats(mids[...])
        ng = nacc[...]
        e = ng * vec_ref[1:2, :]
        cf = cot.astype(F32)
        back = e - jnp.mean(e, axis=1, keepdims=True) - xh * jnp.mean(e * xh, axis=1, keepdims=True)
        mg = cf + r * back
        mg_ref[...] = mg
        bg = mg.astype(BF)
        atg_ref[...] = nt(bg, ow_ref[...]).astype(BF)
        og_ref[...] = tn(att_ref[...], bg).astype(BF)

        def total(a):
            return jnp.sum(a, axis=0, keepdims=True)

        z = jnp.zeros((4, vg_ref.shape[1]), F32)
        vg_ref[...] = jnp.concatenate(
            [total(bg.astype(F32)), total(ng * xh), total(ng), total(cf), z], axis=0
        )


def ffn(x, att, cot, ow, vec, up, upb, dn, fb=512):
    R, D = x.shape
    F = up.shape[1]
    nf = F // fb
    S = jax.ShapeDtypeStruct

    def full(a):
        return pl.BlockSpec(a.shape, lambda f: (0,) * len(a.shape))

    outs = [
        S((R, D), BF),
        S((R, D), F32),
        S((R, D), BF),
        S((D, F), BF),
        S((F, D), BF),
        S((D, D), BF),
        S((8, D), F32),
        S((1, F), F32),
    ]
    colb = pl.BlockSpec((D, fb), lambda f: (0, f))
    rowb = pl.BlockSpec((fb, D), lambda f: (f, 0))
    vecb = pl.BlockSpec((1, fb), lambda f: (0, f))
    return pl.pallas_call(
        functools.partial(ffn_kernel, nf),
        grid=(nf,),
        in_specs=[full(x), full(att), full(cot), full(ow), full(vec), colb, vecb, rowb],
        out_specs=[full(o) for o in outs[:3]] + [colb, rowb, full(outs[5]), full(outs[6]), vecb],
        out_shape=outs,
        scratch_shapes=[
            pltpu.VMEM((R, D), F32),
            pltpu.VMEM((R, D), BF),
            pltpu.VMEM((D, R), BF),
            pltpu.VMEM((D, R), BF),
            pltpu.VMEM((R, D), F32),
            pltpu.VMEM((R, D), F32),
        ],
        compiler_params=pltpu.CompilerParams(vmem_limit_bytes=VMEM_LIMIT),
        cost_estimate=pl.CostEstimate(
            flops=12 * R * D * F, bytes_accessed=16 * R * D, transcendentals=R * F
        ),
        name="ffn",
    )(x, att, cot, ow, vec, up, upb, dn)


def per_device(
    tokens_in,
    norm1_gain,
    norm1_bias,
    qkv_weight,
    qkv_bias,
    out_weight,
    out_bias,
    norm2_gain,
    norm2_bias,
    up_weight,
    up_bias,
    down_weight,
    down_bias,
    cotangent,
    long_slot,
):
    n = lax.axis_size("head")
    nb = lax.axis_size("batch")
    me = lax.axis_index("head")
    bi = lax.axis_index("batch")
    slots = long_slot.shape[0]
    g = n // slots
    p = me % g
    R, D = tokens_in.shape
    L = R * g
    W = qkv_weight.shape[2]
    FS = up_weight.shape[1]
    flag = lax.dynamic_slice(long_slot, (me // g,), (1,))

    def cross(x, r):
        return lax.ppermute(x, "head", [(i, (i + r * g) % n) for i in range(n)])

    def rot(x, r):
        return lax.ppermute(x, "head", [(i, i // g * g + (i % g - r) % g) for i in range(n)])

    def flip(x, bit):
        return lax.ppermute(x, "batch", [(i, i ^ bit) for i in range(nb)])

    def phases(x):
        return [x] + [cross(x, r) for r in range(1, slots)]

    def group(x):
        return [x] + [rot(x, r) for r in range(1, g)]

    def rows_of(x, member):
        return lax.dynamic_slice_in_dim(x, member * R, R, 0)

    qw = phases(qkv_weight.reshape(D, 3 * W))
    ow = phases(out_weight)
    uw = phases(up_weight)
    dw = phases(down_weight)
    qb = phases(qkv_bias.reshape(3, 1, W))
    ub = phases(up_bias.reshape(1, FS))

    x = tokens_in.astype(F32)
    gain1 = norm1_gain.astype(F32)
    xh1, r1 = ln_stats(x)
    n1 = (xh1 * gain1 + norm1_bias.astype(F32)).astype(BF)
    pieces = group(n1)
    n1all = jnp.zeros((L, D), BF)
    for r in range(g):
        n1all = lax.dynamic_update_slice_in_dim(n1all, pieces[r], (p + r) % g * R, 0)

    att_cols = []
    saved = []
    for ph in range(slots):
        w3 = qw[ph].reshape(D, 3, W)
        q, k, v = (
            (nn(n1all, w3[:, i]) + qb[ph][i].astype(F32)).astype(BF) for i in range(3)
        )
        o, st, ws = attn_fwd(flag, q, k, v)
        saved.append((q, k, v, o, st, ws))
        cols = [None] * g
        cols[0] = rows_of(o, p)
        for r in range(1, g):
            cols[r] = rot(rows_of(o, (p - r) % g), r)
        att_cols += cols
    att = jnp.concatenate(att_cols, axis=1)

    owf = jnp.concatenate([b for a in ow for b in group(a)], axis=0)
    uwf = jnp.concatenate([b for a in uw for b in group(a)], axis=1)
    dwf = jnp.concatenate([b for a in dw for b in group(a)], axis=0)
    ubf = jnp.concatenate([b for a in ub for b in group(a)], axis=1).astype(F32)
    vec = jnp.stack([out_bias, norm2_gain, norm2_bias, down_bias] + [out_bias] * 4).astype(F32)
    layer_out, mg, atg, ug, dg, og, vg, ubg = ffn(
        tokens_in, att, cotangent, owf, vec, uwf, ubf, dwf
    )

    def reduce_batch(a):
        bits = []
        bit = 1
        while bit < nb:
            bits.append(bit)
            bit *= 2
        for bit in bits:
            half = a.shape[0] // 2
            up_side = (bi & bit) > 0
            lo_half, hi_half = a[:half], a[half:]
            got = flip(jnp.where(up_side, lo_half, hi_half), bit)
            keep = jnp.where(up_side, hi_half, lo_half)
            a = (keep.astype(F32) + got.astype(F32)).astype(BF)
        for bit in bits[::-1]:
            up_side = (bi & bit) > 0
            got = flip(a, bit)
            a = jnp.concatenate([jnp.where(up_side, got, a), jnp.where(up_side, a, got)], axis=0)
        return a

    def reduce_group(parts):
        out = []
        for ph in range(slots):
            a = parts[ph][0].astype(F32)
            for r in range(1, g):
                a = a + rot(parts[ph][r], g - r).astype(F32)
            out.append(a.astype(BF))
        return out

    def reduce_cross(parts):
        a = parts[0].astype(F32)
        for r in range(1, slots):
            a = a + cross(parts[r], slots - r).astype(F32)
        return a.astype(BF)

    def cols(a, i, w):
        return a[:, i * w : (i + 1) * w]

    def rows(a, i, w):
        return a[i * w : (i + 1) * w]

    ug_own = reduce_batch(
        reduce_cross(
            reduce_group([[cols(ug, ph * g + r, FS) for r in range(g)] for ph in range(slots)])
        )
    )
    dg_own = reduce_batch(
        reduce_cross(
            reduce_group(
                [
                    [
                        jnp.concatenate([rows(dg, ph * g + r, FS), rows(og, ph * g + r, W)], 0)
                        for r in range(g)
                    ]
                    for ph in range(slots)
                ]
            )
        )
    )

    n1g = jnp.zeros((L, D), F32)
    qg_parts = []
    qbg_parts = []
    for ph in range(slots):
        q, k, v, o, st, ws = saved[ph]
        mine = [cols(atg, ph * g + r, W) for r in range(g)]
        do = jnp.zeros((L, W), BF)
        do = lax.dynamic_update_slice_in_dim(do, mine[0], p * R, 0)
        for r in range(1, g):
            do = lax.dynamic_update_slice_in_dim(do, rot(mine[r], g - r), (p - r) % g * R, 0)
        tg = jnp.concatenate(attn_bwd(flag, q, k, v, o, do, st, ws), axis=1)
        qg_parts.append(tn(n1all, tg).astype(BF))
        qbg_parts.append(jnp.sum(tg.astype(F32), axis=0))
        n1g = n1g + nt(tg, qw[ph])
    qg_own = reduce_batch(reduce_cross(qg_parts))

    ng = rows_of(n1g, p)
    for r in range(1, g):
        ng = ng + rot(rows_of(n1g, (p - r) % g).astype(BF), r).astype(F32)
    e = ng * gain1
    back = e - jnp.mean(e, axis=1, keepdims=True) - xh1 * jnp.mean(e * xh1, axis=1, keepdims=True)
    input_grad = (mg + r1 * back).astype(BF)

    shard_w = 3 * W + FS
    shard_vec = jnp.zeros((n, shard_w), F32)
    for ph in range(slots):
        owner = (me - ph * g) % n
        own_row = jnp.concatenate([qbg_parts[ph], jnp.zeros((FS,), F32)])
        shard_vec = lax.dynamic_update_slice(shard_vec, own_row[None], (owner, 0))
        for r in range(g):
            shard = (me - ph * g) % n // g * g + (p + r) % g
            shard_vec = lax.dynamic_update_slice(
                shard_vec, cols(ubg, ph * g + r, FS), (shard, 3 * W)
            )
    small = jnp.concatenate(
        [shard_vec.reshape(-1), vg[:4].reshape(-1), jnp.sum(ng * xh1, 0), jnp.sum(ng, 0)]
    ).reshape(-1, 128)
    bit = 1
    while bit < n:
        small = small + lax.ppermute(small, "head", [(i, i ^ bit) for i in range(n)])
        bit *= 2
    bit = 1
    while bit < nb:
        small = small + flip(small, bit)
        bit *= 2
    small = small.reshape(-1)
    shard_sum = lax.dynamic_slice(small[: n * shard_w].reshape(n, shard_w), (me, 0), (1, shard_w))[0]
    vs = small[n * shard_w :].reshape(6, D)
    return (
        layer_out,
        input_grad,
        vs[4],
        vs[5],
        qg_own.astype(F32).reshape(D, 3, W),
        shard_sum[: 3 * W].reshape(3, W),
        dg_own[FS:].astype(F32),
        vs[0],
        vs[1],
        vs[2],
        ug_own.astype(F32),
        shard_sum[3 * W :],
        dg_own[:FS].astype(F32),
        vs[3],
    )


def solution(mesh):
    rows = P(("batch", "head"), None)
    return jax.shard_map(
        per_device,
        mesh=mesh,
        in_specs=(
            rows,
            P(),
            P(),
            P(None, None, "head"),
            P(None, "head"),
            P("head", None),
            P(),
            P(),
            P(),
            P(None, "head"),
            P("head"),
            P("head", None),
            P(),
            rows,
            P("batch"),
        ),
        out_specs=(
            rows,
            rows,
            P(),
            P(),
            P(None, None, "head"),
            P(None, "head"),
            P("head", None),
            P(),
            P(),
            P(),
            P(None, "head"),
            P("head"),
            P("head", None),
            P(),
        ),
        check_vma=False,
    )
```

time: 1090 us -> 291 us (0.27)
  matrix products: 426 us -> 14.2 us
  waiting for transfers between devices: 416 us -> 73.6 us
  Pallas kernels: 0 us -> 77.6 us
  blocking collectives: 61.4 us -> 0 us
  starting transfers between devices: 0.95 us -> 55.3 us
  other arithmetic: 71.1 us -> 30.6 us
  loops' own time: 38.5 us -> 0 us
  between operations: 16.7 us -> 1.82 us
  local copies, waits for them, and re-layouts: 47 us -> 32.3 us
    dot_general x62 -> x10, matrix products: 426 us -> 14.2 us  [the longest x6 9.13 us: nn(): lax.dot_general(a, b, (((1,), (0,)), ((), ())), preferred_element_type=F32)]
    reduce_scatter x4 -> x0, waiting for transfers between devices: 242 us -> none  [the longest x1 70.6 us: per_device(): lax.psum_scatter(jnp.dot(picked, out_weight, preferred_element_type=jnp.f...]
    all_gather x4 -> x0, waiting for transfers between devices: 114 us -> none  [the longest x1 34.1 us: per_device(): gathered1 = lax.all_gather(normed1, 'head', axis=0, tiled=True)]
    pallas_call x0 -> x5, Pallas kernels: none -> 77.6 us  [the longest x2 30.1 us: attn_bwd(): pl.pallas_call(functools.partial(bwd_kernel, bq, bk, nh, W, L), grid=(L /...]
    ppermute x0 -> x50, waiting for transfers between devices: none -> 73.6 us  [the longest x9 36.9 us: cross(): return lax.ppermute(x, 'head', [(i, (i + r * g) % n) for i in range(n)])]
    psum x2 -> x0, blocking collectives: 61.4 us -> none  [the longest x1 39.5 us: per_device(): lax.psum((first_gain_grad, first_bias_grad, out_bias_local, second_gain_g...]
    psum x1 -> x0, waiting for transfers between devices: 59.2 us -> none  [per_device(): lax.psum(qkv_grad.astype(jnp.bfloat16), 'batch').astype(jnp.float32)]
    ppermute x0 -> x50, starting transfers between devices: none -> 55.3 us  [the longest x21 40.1 us: flip(): return lax.ppermute(x, 'batch', [(i, i ^ bit) for i in range(nb)])]
  transfers between devices with their start and end apart: 9 -> 50, of which waited for: 9 -> 23; matrix products, arithmetic and copies ran while one was open for 5% -> 22% of each run, Pallas kernels for 0% -> 18%
where the time goes in v1:
time: 291 us; the launch traced here: 285 us
  Pallas kernels  77.6 us (27%)
  waiting for transfers between devices  73.6 us (25%)
  starting transfers between devices  55.3 us (19%)
  local copies, waits for them, and re-layouts  32.3 us (11%)
  other arithmetic  30.6 us (11%)
  matrix products  14.2 us (5%)
    ppermute x21, starting transfers between devices, flip(): return lax.ppermute(x, 'batch', [(i, i ^ bit) for i in range(nb)])  40.1 us
    ppermute x9, waiting for transfers between devices, cross(): return lax.ppermute(x, 'head', [(i, (i + r * g) % n) for i in range(n)])  36.9 us
    ppermute x21, waiting for transfers between devices, flip(): return lax.ppermute(x, 'batch', [(i, i ^ bit) for i in range(nb)])  31.6 us
    pallas_call x2, Pallas kernels, attn_bwd(): pl.pallas_call(functools.partial(bwd_kernel, bq, bk, nh, W, L), grid=(L /...  30.1 us
    pallas_call x1, Pallas kernels, ffn(): pl.pallas_call(functools.partial(ffn_kernel, nf), grid=(nf,), in_specs=[f...  25.8 us
    pallas_call x2, Pallas kernels, attn_fwd(): pl.pallas_call(functools.partial(fwd_kernel, bq, bk, nh, W, L), grid=(L /...  21.7 us
    ppermute x9, starting transfers between devices, cross(): return lax.ppermute(x, 'head', [(i, (i + r * g) % n) for i in range(n)])  10.8 us
    dot_general x6, matrix products, nn(): lax.dot_general(a, b, (((1,), (0,)), ((), ())), preferred_element_type=F32)  9.13 us
  transfers between devices with their start and end apart: 50, of which 23 were waited for; matrix products, arithmetic and copies ran while one was open for 22% of the time, Pallas kernels for 18%

profile of v1, /device:TPU:0, one launch (start us, length us, event | category | flops | bytes accessed | tf_op | source)
XLA Modules:
  0.0 285.5 jit_solution(18215989919393263472)
XLA Ops:
  0.7 1.5 convert_reduce_fusion.2
  2.3 1.7 fusion.20
  6.2 2.6 collective-permute-start.12
  9.3 1.7 collective-permute-start.9
  16.9 1.7 collective-permute-start.6
  20.0 17.4 %collective-permute-done.6 = bf16[128,512]{1,0:T(8,128)(2,1)S(1)} collective-permute-done((bf16[128,512]{1,0:T(8,128)(2,1)}, bf16[128,512]{1,0:T(8,128)(2,1)S(1)}, u32[]{:S(2)}, u32[]{:S(2)}) %collective-permute-start.6) | collective-permute-done | bytes 131104 | tf_op jit(solution)/shard_map/ppermute | solution.py:491
  38.9 1.7 pad_maximum_fusion.6.ow_ref
  40.7 1.7 collective-permute-start.2
  44.2 1.5 fusion.6.q_ref
  45.7 1.5 fusion.7.k_ref
  47.3 1.6 fusion.8.v_ref
  48.8 10.8 %attn_fwd.2 = (bf16[2048,128]{1,0:T(8,128)(2,1)}, f32[2048,128]{1,0:T(8,128)}, bf16[2,2048,512]{2,1,0:T(8,128)(2,1)}, bf16[2,2048,512]{2,1,0:T(8,128)(2,1)}, bf1...) custom-call(s32[1]{0:T(128)} %dynamic_slice.24.flag_ref, bf16[2048,128]{1,0:T(8,128)(2,1)} %fusion.6.q_ref, ...), custom_call_target="tpu_custom_call" | custom-call | flops 4294967296 | bytes 16777216 | tf_op jit(solution)/shard_map/attn_fwd/pallas_call | solution.py:198
  62.4 1.5 fusion.11.v_ref
  63.9 1.5 fusion.9.q_ref
  65.4 10.8 %attn_fwd.3 = (bf16[2048,128]{1,0:T(8,128)(2,1)}, f32[2048,128]{1,0:T(8,128)}, bf16[2,2048,512]{2,1,0:T(8,128)(2,1)}, bf16[2,2048,512]{2,1,0:T(8,128)(2,1)}, bf1...) custom-call(s32[1]{0:T(128)} %dynamic_slice.24.flag_ref, bf16[2048,128]{1,0:T(8,128)(2,1)} %fusion.9.q_ref, ...), custom_call_target="tpu_custom_call" | custom-call | flops 4294967296 | bytes 16777216 | tf_op jit(solution)/shard_map/attn_fwd/pallas_call | solution.py:198
  77.9 2.7 pad_maximum_fusion.up_ref
  83.1 25.8 %ffn.1 = (bf16[1024,512]{1,0:T(8,128)(2,1)}, f32[1024,512]{1,0:T(8,128)}, bf16[1024,512]{1,0:T(8,128)(2,1)}, bf16[512,2048]{1,0:T(8,128)(2,1)}, bf16[2048,512]{1...) custom-call(bf16[1024,512]{1,0:T(8,128)(2,1)} %x_ref.1, ...), custom_call_target="tpu_custom_call" | custom-call | flops 12884901888 | bytes 8388608 | tf_op jit(solution)/shard_map/ffn/pallas_call | solution.py:438
  109.0 1.8 fusion.35
  118.9 14.9 %attn_bwd.2 = (bf16[2048,128]{1,0:T(8,128)(2,1)}, bf16[2048,128]{1,0:T(8,128)(2,1)}, bf16[2048,128]{1,0:T(8,128)(2,1)}) custom-call(s32[1]{0:T(128)} %dynamic_slice.24.flag_ref, bf16[2048,128]{1,0:T(8,128)(2,1)} %fusion.6.q_ref, bf16[2048,128]{1,0:T(8,128)(2,1)} %fusion.7.k_ref, bf16[2048,128]{1,0:T(8,128)(2,1)} %fusion.8.v_ref, ...), custom_call_target="tpu_custom_call" | custom-call | flops 8589934592 | bytes 16777216 | tf_op jit(solution)/shard_map/attn_bwd/pallas_call | solution.py:302
  135.7 15.3 %attn_bwd.3 = (bf16[2048,128]{1,0:T(8,128)(2,1)}, bf16[2048,128]{1,0:T(8,128)(2,1)}, bf16[2048,128]{1,0:T(8,128)(2,1)}) custom-call(s32[1]{0:T(128)} %dynamic_slice.24.flag_ref, bf16[2048,128]{1,0:T(8,128)(2,1)} %fusion.9.q_ref, bf16[2048,128]{1,0:T(8,128)(2,1)} %fusion.10.k_ref, bf16[2048,128]{1,0:T(8,128)(2,1)} %fusion.11.v_ref, ...), custom_call_target="tpu_custom_call" | custom-call | flops 8589934592 | bytes 16777216 | tf_op jit(solution)/shard_map/attn_bwd/pallas_call | solution.py:302
  158.3 7.9 %collective-permute-done.25 = bf16[512,384]{1,0:T(8,128)(2,1)S(1)} collective-permute-done((bf16[512,384]{1,0:T(8,128)(2,1)S(1)}, bf16[512,384]{1,0:T(8,128)(2,1)S(1)}, u32[]{:S(2)}, u32[]{:S(2)}) %collective-permute-start.25) | collective-permute-done | bytes 393248 | tf_op jit(solution)/shard_map/ppermute | solution.py:491
  168.3 13.4 %collective-permute-start.26 = (bf16[256,384]{1,0:T(8,128)(2,1)}, bf16[256,384]{1,0:T(8,128)(2,1)}, u32[]{:S(2)}, u32[]{:S(2)}) collective-permute-start(bf16[256,384]{1,0:T(8,128)(2,1)} %broadcast_select_fusion.8), channel_id=1, source_target_pairs={{0,4},{4,0},{8,12},{12,8},{16,20},{20,16},{24,28},{28,24},{1,5},{5... | collective-permute-start | bytes 589832 | tf_op jit(solution)/shard_map/ppermute | solution.py:497
  193.6 1.6 collective-permute-start.27
  196.4 2.4 collective-permute-done.27
  199.2 2.9 %collective-permute-start.28 = (bf16[64,384]{1,0:T(8,128)(2,1)S(1)}, bf16[64,384]{1,0:T(8,128)(2,1)S(1)}, u32[]{:S(2)}, u32[]{:S(2)}) collective-permute-start(bf16[64,384]{1,0:T(8,128)(2,1)S(1)} %broadcast_select_fusion.26), channel_id=1, source_target_pairs={{0,16},{4,20},{8,24},{12,28},{16,0},{20,4},{24,8},{28,12},{1,17},{... | collective-permute-start | bytes 147464 | tf_op jit(solution)/shard_map/ppermute | solution.py:497
  204.3 1.7 collective-permute-start.34
  206.0 2.7 collective-permute-start.29
  208.7 4.9 %collective-permute-done.43 = bf16[512,512]{1,0:T(8,128)(2,1)S(1)} collective-permute-done((bf16[512,512]{1,0:T(8,128)(2,1)S(1)}, bf16[512,512]{1,0:T(8,128)(2,1)S(1)}, u32[]{:S(2)}, u32[]{:S(2)}) %collective-permute-start.43) | collective-permute-done | bytes 524320 | tf_op jit(solution)/shard_map/ppermute | solution.py:491
  215.0 1.6 collective-permute-start.30
  216.8 2.9 %collective-permute-done.30 = bf16[128,384]{1,0:T(8,128)(2,1)S(1)} collective-permute-done((bf16[128,384]{1,0:T(8,128)(2,1)S(1)}, bf16[128,384]{1,0:T(8,128)(2,1)S(1)}, u32[]{:S(2)}, u32[]{:S(2)}) %collective-permute-start.30) | collective-permute-done | bytes 98336 | tf_op jit(solution)/shard_map/ppermute | solution.py:497
  219.9 6.6 %collective-permute-done.34 = bf16[640,512]{1,0:T(8,128)(2,1)S(1)} collective-permute-done((bf16[640,512]{1,0:T(8,128)(2,1)S(1)}, bf16[640,512]{1,0:T(8,128)(2,1)S(1)}, u32[]{:S(2)}, u32[]{:S(2)}) %collective-permute-start.34) | collective-permute-done | bytes 655392 | tf_op jit(solution)/shard_map/ppermute | solution.py:491
  228.2 1.6 collective-permute-start.45
  229.9 1.5 fusion.19
  233.1 1.9 fusion.18
  235.0 1.7 collective-permute-done.21
  236.7 2.1 collective-permute-start.22
  242.3 2.2 collective-permute-done.23
  244.5 2.6 collective-permute-start.24
  247.6 2.0 collective-permute-done.24
  253.3 1.8 collective-permute-start.47
  255.0 2.9 %collective-permute-done.36 = bf16[160,512]{1,0:T(8,128)(2,1)S(1)} collective-permute-done((bf16[160,512]{1,0:T(8,128)(2,1)S(1)}, bf16[160,512]{1,0:T(8,128)(2,1)S(1)}, u32[]{:S(2)}, u32[]{:S(2)}) %collective-permute-start.36) | collective-permute-done | bytes 163872 | tf_op jit(solution)/shard_map/ppermute | solution.py:497
  258.0 2.0 collective-permute-start.37
  260.0 4.6 %collective-permute-done.37 = bf16[80,512]{1,0:T(8,128)(2,1)S(1)} collective-permute-done((bf16[80,512]{1,0:T(8,128)(2,1)S(1)}, bf16[80,512]{1,0:T(8,128)(2,1)S(1)}, u32[]{:S(2)}, u32[]{:S(2)}) %collective-permute-start.37) | collective-permute-done | bytes 81952 | tf_op jit(solution)/shard_map/ppermute | solution.py:497
  265.5 2.0 collective-permute-start.48
  267.5 3.1 %collective-permute-done.38 = bf16[80,512]{1,0:T(8,128)(2,1)S(1)} collective-permute-done((bf16[80,512]{1,0:T(8,128)(2,1)S(1)}, bf16[80,512]{1,0:T(8,128)(2,1)S(1)}, u32[]{:S(2)}, u32[]{:S(2)}) %collective-permute-start.38) | collective-permute-done | bytes 81952 | tf_op jit(solution)/shard_map/ppermute | solution.py:497
  271.5 1.9 collective-permute-start.49
  273.4 2.7 collective-permute-done.39
  279.1 4.2 %collective-permute-done.40 = bf16[320,512]{1,0:T(8,128)(2,1)S(1)} collective-permute-done((bf16[320,512]{1,0:T(8,128)(2,1)S(1)}, bf16[320,512]{1,0:T(8,128)(2,1)S(1)}, u32[]{:S(2)}, u32[]{:S(2)}) %collective-permute-start.40) | collective-permute-done | bytes 327712 | tf_op jit(solution)/shard_map/ppermute | solution.py:497
  (251 shorter events, 74.4 us)
Async XLA Ops:
  5.7 36.8 %collective-permute-start = (bf16[1024,512]{1,0:T(8,128)(2,1)}, bf16[1024,512]{1,0:T(8,128)(2,1)}, u32[]{:S(2)}, u32[]{:S(2)}) collective-permute-start(bf16[1024,512]{1,0:T(8,128)(2,1)} %get-tuple-element.86), channel_id=1, source_target_pairs={{0,1},{1,0},{2,3},{3,2},{4,5},{5,4},{6,7},{7,6},{8,9},{9,8},{10,11... | collective-permute-start | bytes 3145736 | tf_op jit(solution)/shard_map/ppermute | solution.py:494
  6.2 10.8 %collective-permute-start.12 = (bf16[1,512]{1,0:T(2,128)(2,1)S(1)}, bf16[1,512]{1,0:T(2,128)(2,1)S(1)}, u32[]{:S(2)}, u32[]{:S(2)}) collective-permute-start(bf16[1,512]{1,0:T(2,128)(2,1)S(1)} %concatenate.87), channel_id=1, source_target_pairs={{0,2},{1,3},{2,0},{3,1},{4,6},{5,7},{6,4},{7,5},{8,10},{9,11},{10,... | collective-permute-start | bytes 3080 | tf_op jit(solution)/shard_map/ppermute | solution.py:491
  8.8 9.9 %collective-permute-start.11 = (bf16[1,512]{1,0:T(2,128)(2,1)S(1)}, bf16[1,512]{1,0:T(2,128)(2,1)S(1)}, u32[]{:S(2)}, u32[]{:S(2)}) collective-permute-start(bf16[1,512]{1,0:T(2,128)(2,1)S(1)} %concatenate.87), channel_id=1, source_target_pairs={{0,1},{1,0},{2,3},{3,2},{4,5},{5,4},{6,7},{7,6},{8,9},{9,8},{10,11... | collective-permute-start | bytes 3080 | tf_op jit(solution)/shard_map/ppermute | solution.py:494
  8.9 7.7 %collective-permute-start.3 = (bf16[3,1,128]{2,0,1:T(4,128)(2,1)}, bf16[3,1,128]{2,0,1:T(4,128)(2,1)S(1)}, u32[]{:S(2)}, u32[]{:S(2)}) collective-permute-start(bf16[3,1,128]{2,0,1:T(4,128)(2,1)} %bitcast.9), channel_id=1, source_target_pairs={{0,2},{1,3},{2,0},{3,1},{4,6},{5,7},{6,4},{7,5},{8,10},{9,11},{10,... | collective-permute-start | bytes 2312 | tf_op jit(solution)/shard_map/ppermute | solution.py:491
  9.3 31.4 %collective-permute-start.9 = (bf16[512,512]{1,0:T(8,128)(2,1)}, bf16[512,512]{1,0:T(8,128)(2,1)S(1)}, u32[]{:S(2)}, u32[]{:S(2)}) collective-permute-start(bf16[512,512]{1,0:T(8,128)(2,1)} %param.24), channel_id=1, source_target_pairs={{0,2},{1,3},{2,0},{3,1},{4,6},{5,7},{6,4},{7,5},{8,10},{9,11},{10,... | collective-permute-start | bytes 1572872 | tf_op jit(solution)/shard_map/ppermute | solution.py:491
  16.6 25.8 %collective-permute-start.15 = (bf16[512,512]{1,0:T(8,128)(2,1)}, bf16[512,512]{1,0:T(8,128)(2,1)S(1)}, u32[]{:S(2)}, u32[]{:S(2)}) collective-permute-start(bf16[512,512]{1,0:T(8,128)(2,1)} %param.26), channel_id=1, source_target_pairs={{0,2},{1,3},{2,0},{3,1},{4,6},{5,7},{6,4},{7,5},{8,10},{9,11},{10,... | collective-permute-start | bytes 1572872 | tf_op jit(solution)/shard_map/ppermute | solution.py:491
  16.9 20.5 %collective-permute-start.6 = (bf16[128,512]{1,0:T(8,128)(2,1)}, bf16[128,512]{1,0:T(8,128)(2,1)S(1)}, u32[]{:S(2)}, u32[]{:S(2)}) collective-permute-start(bf16[128,512]{1,0:T(8,128)(2,1)} %param.20), channel_id=1, source_target_pairs={{0,2},{1,3},{2,0},{3,1},{4,6},{5,7},{6,4},{7,5},{8,10},{9,11},{10,... | collective-permute-start | bytes 393224 | tf_op jit(solution)/shard_map/ppermute | solution.py:491
  19.8 18.2 %collective-permute-start.5 = (bf16[128,512]{1,0:T(8,128)(2,1)}, bf16[128,512]{1,0:T(8,128)(2,1)S(1)}, u32[]{:S(2)}, u32[]{:S(2)}) collective-permute-start(bf16[128,512]{1,0:T(8,128)(2,1)} %param.20), channel_id=1, source_target_pairs={{0,1},{1,0},{2,3},{3,2},{4,5},{5,4},{6,7},{7,6},{8,9},{9,8},{10,11... | collective-permute-start | bytes 393224 | tf_op jit(solution)/shard_map/ppermute | solution.py:494
  37.4 1.3 collective-permute-start.7
  38.0 39.3 %collective-permute-start.8 = (bf16[512,512]{1,0:T(8,128)(2,1)}, bf16[512,512]{1,0:T(8,128)(2,1)S(1)}, u32[]{:S(2)}, u32[]{:S(2)}) collective-permute-start(bf16[512,512]{1,0:T(8,128)(2,1)} %param.24), channel_id=1, source_target_pairs={{0,1},{1,0},{2,3},{3,2},{4,5},{5,4},{6,7},{7,6},{8,9},{9,8},{10,11... | collective-permute-start | bytes 1572872 | tf_op jit(solution)/shard_map/ppermute | solution.py:494
  38.8 41.8 %collective-permute-start.14 = (bf16[512,512]{1,0:T(8,128)(2,1)}, bf16[512,512]{1,0:T(8,128)(2,1)S(1)}, u32[]{:S(2)}, u32[]{:S(2)}) collective-permute-start(bf16[512,512]{1,0:T(8,128)(2,1)} %param.26), channel_id=1, source_target_pairs={{0,1},{1,0},{2,3},{3,2},{4,5},{5,4},{6,7},{7,6},{8,9},{9,8},{10,11... | collective-permute-start | bytes 1572872 | tf_op jit(solution)/shard_map/ppermute | solution.py:494
  40.7 20.1 %collective-permute-start.2 = (bf16[512,384]{0,1:T(8,128)(2,1)S(1)}, bf16[512,384]{0,1:T(8,128)(2,1)S(1)}, u32[]{:S(2)}, u32[]{:S(2)}) collective-permute-start(bf16[512,384]{0,1:T(8,128)(2,1)S(1)} %bitcast.84), channel_id=1, source_target_pairs={{0,2},{1,3},{2,0},{3,1},{4,6},{5,7},{6,4},{7,5},{8,10},{9,11},{10,... | collective-permute-start | bytes 1179656 | tf_op jit(solution)/shard_map/ppermute | solution.py:491
  42.4 35.5 %collective-permute-start.10 = (bf16[512,512]{1,0:T(8,128)(2,1)S(1)}, bf16[512,512]{1,0:T(8,128)(2,1)S(1)}, u32[]{:S(2)}, u32[]{:S(2)}) collective-permute-start(bf16[512,512]{1,0:T(8,128)(2,1)S(1)} %collective-permute-done.9), channel_id=1, source_target_pairs={{0,1},{1,0},{2,3},{3,2},{4,5},{5,4},{6,7},{7,6},{8,9},{9,8},{10,11... | collective-permute-start | bytes 1572872 | tf_op jit(solution)/shard_map/ppermute | solution.py:494
  42.5 38.1 %collective-permute-start.16 = (bf16[512,512]{1,0:T(8,128)(2,1)S(1)}, bf16[512,512]{1,0:T(8,128)(2,1)S(1)}, u32[]{:S(2)}, u32[]{:S(2)}) collective-permute-start(bf16[512,512]{1,0:T(8,128)(2,1)S(1)} %collective-permute-done.15), channel_id=1, source_target_pairs={{0,1},{1,0},{2,3},{3,2},{4,5},{5,4},{6,7},{7,6},{8,9},{9,8},{10,11... | collective-permute-start | bytes 1572872 | tf_op jit(solution)/shard_map/ppermute | solution.py:494
  60.7 21.3 %collective-permute-start.1 = (bf16[1024,128]{1,0:T(8,128)(2,1)S(1)}, bf16[1024,128]{1,0:T(8,128)(2,1)S(1)}, u32[]{:S(2)}, u32[]{:S(2)}) collective-permute-start(bf16[1024,128]{1,0:T(8,128)(2,1)S(1)} %get-tuple-element.105), channel_id=1, source_target_pairs={{0,1},{1,0},{2,3},{3,2},{4,5},{5,4},{6,7},{7,6},{8,9},{9,8},{10,11... | collective-permute-start | bytes 786440 | tf_op jit(solution)/shard_map/ppermute | solution.py:494
  77.3 4.7 %collective-permute-start.4 = (bf16[1024,128]{1,0:T(8,128)(2,1)S(1)}, bf16[1024,128]{1,0:T(8,128)(2,1)S(1)}, u32[]{:S(2)}, u32[]{:S(2)}) collective-permute-start(bf16[1024,128]{1,0:T(8,128)(2,1)S(1)} %get-tuple-element.107), channel_id=1, source_target_pairs={{0,1},{1,0},{2,3},{3,2},{4,5},{5,4},{6,7},{7,6},{8,9},{9,8},{10,11... | collective-permute-start | bytes 786440 | tf_op jit(solution)/shard_map/ppermute | solution.py:494
  112.4 107.5 %collective-permute-start.32 = (bf16[640,512]{1,0:T(8,128)(2,1)}, bf16[640,512]{1,0:T(8,128)(2,1)}, u32[]{:S(2)}, u32[]{:S(2)}) collective-permute-start(bf16[640,512]{1,0:T(8,128)(2,1)} %pad_maximum_fusion.3), channel_id=1, source_target_pairs={{0,1},{1,0},{2,3},{3,2},{4,5},{5,4},{6,7},{7,6},{8,9},{9,8},{10,11... | collective-permute-start | bytes 1966088 | tf_op jit(solution)/shard_map/ppermute | solution.py:494
  113.3 85.9 %collective-permute-start.33 = (bf16[640,512]{1,0:T(8,128)(2,1)}, bf16[640,512]{1,0:T(8,128)(2,1)}, u32[]{:S(2)}, u32[]{:S(2)}) collective-permute-start(bf16[640,512]{1,0:T(8,128)(2,1)} %pad_maximum_fusion.4), channel_id=1, source_target_pairs={{0,1},{1,0},{2,3},{3,2},{4,5},{5,4},{6,7},{7,6},{8,9},{9,8},{10,11... | collective-permute-start | bytes 1966088 | tf_op jit(solution)/shard_map/ppermute | solution.py:494
  114.8 78.7 %collective-permute-start.42 = (bf16[512,512]{1,0:T(8,128)(2,1)}, bf16[512,512]{1,0:T(8,128)(2,1)}, u32[]{:S(2)}, u32[]{:S(2)}) collective-permute-start(bf16[512,512]{1,0:T(8,128)(2,1)} %get-tuple-element.88), channel_id=1, source_target_pairs={{0,1},{1,0},{2,3},{3,2},{4,5},{5,4},{6,7},{7,6},{8,9},{9,8},{10,11... | collective-permute-start | bytes 1572872 | tf_op jit(solution)/shard_map/ppermute | solution.py:494
  114.9 91.1 %collective-permute-start.41 = (bf16[512,512]{1,0:T(8,128)(2,1)}, bf16[512,512]{1,0:T(8,128)(2,1)}, u32[]{:S(2)}, u32[]{:S(2)}) collective-permute-start(bf16[512,512]{1,0:T(8,128)(2,1)} %get-tuple-element.87), channel_id=1, source_target_pairs={{0,1},{1,0},{2,3},{3,2},{4,5},{5,4},{6,7},{7,6},{8,9},{9,8},{10,11... | collective-permute-start | bytes 1572872 | tf_op jit(solution)/shard_map/ppermute | solution.py:494
  115.6 2.3 collective-permute-start.17
  117.9 17.0 %collective-permute-start.18 = (bf16[1024,128]{1,0:T(8,128)(2,1)S(1)}, bf16[1024,128]{1,0:T(8,128)(2,1)S(1)}, u32[]{:S(2)}, u32[]{:S(2)}) collective-permute-start(bf16[1024,128]{1,0:T(8,128)(2,1)S(1)} %get-tuple-element.94), channel_id=1, source_target_pairs={{0,1},{1,0},{2,3},{3,2},{4,5},{5,4},{6,7},{7,6},{8,9},{9,8},{10,11... | collective-permute-start | bytes 786440 | tf_op jit(solution)/shard_map/ppermute | solution.py:494
  154.8 11.5 %collective-permute-start.25 = (bf16[512,384]{1,0:T(8,128)(2,1)S(1)}, bf16[512,384]{1,0:T(8,128)(2,1)S(1)}, u32[]{:S(2)}, u32[]{:S(2)}) collective-permute-start(bf16[512,384]{1,0:T(8,128)(2,1)S(1)} %convolution_convert_fusion), channel_id=1, source_target_pairs={{0,2},{1,3},{2,0},{3,1},{4,6},{5,7},{6,4},{7,5},{8,10},{9,11},{10,... | collective-permute-start | bytes 1179656 | tf_op jit(solution)/shard_map/ppermute | solution.py:491
  168.3 24.2 %collective-permute-start.26 = (bf16[256,384]{1,0:T(8,128)(2,1)}, bf16[256,384]{1,0:T(8,128)(2,1)}, u32[]{:S(2)}, u32[]{:S(2)}) collective-permute-start(bf16[256,384]{1,0:T(8,128)(2,1)} %broadcast_select_fusion.8), channel_id=1, source_target_pairs={{0,4},{4,0},{8,12},{12,8},{16,20},{20,16},{24,28},{28,24},{1,5},{5... | collective-permute-start | bytes 589832 | tf_op jit(solution)/shard_map/ppermute | solution.py:497
  192.5 37.4 %collective-permute-start.19 = (bf16[1024,512]{1,0:T(8,128)(2,1)}, bf16[1024,512]{1,0:T(8,128)(2,1)S(1)}, u32[]{:S(2)}, u32[]{:S(2)}) collective-permute-start(bf16[1024,512]{1,0:T(8,128)(2,1)} %dynamic-slice_convert_fusion), channel_id=1, source_target_pairs={{0,1},{1,0},{2,3},{3,2},{4,5},{5,4},{6,7},{7,6},{8,9},{9,8},{10,11... | collective-permute-start | bytes 3145736 | tf_op jit(solution)/shard_map/ppermute | solution.py:494
  193.6 5.3 %collective-permute-start.27 = (bf16[128,384]{1,0:T(8,128)(2,1)S(1)}, bf16[128,384]{1,0:T(8,128)(2,1)S(1)}, u32[]{:S(2)}, u32[]{:S(2)}) collective-permute-start(bf16[128,384]{1,0:T(8,128)(2,1)S(1)} %broadcast_select_fusion.17), channel_id=1, source_target_pairs={{0,8},{4,12},{8,0},{12,4},{16,24},{20,28},{24,16},{28,20},{1,9},{5... | collective-permute-start | bytes 294920 | tf_op jit(solution)/shard_map/ppermute | solution.py:497
  198.8 14.8 %collective-permute-start.43 = (bf16[512,512]{1,0:T(8,128)(2,1)S(1)}, bf16[512,512]{1,0:T(8,128)(2,1)S(1)}, u32[]{:S(2)}, u32[]{:S(2)}) collective-permute-start(bf16[512,512]{1,0:T(8,128)(2,1)S(1)} %add_convert_fusion.4), channel_id=1, source_target_pairs={{0,2},{1,3},{2,0},{3,1},{4,6},{5,7},{6,4},{7,5},{8,10},{9,11},{10,... | collective-permute-start | bytes 1572872 | tf_op jit(solution)/shard_map/ppermute | solution.py:491
  199.2 5.1 %collective-permute-start.28 = (bf16[64,384]{1,0:T(8,128)(2,1)S(1)}, bf16[64,384]{1,0:T(8,128)(2,1)S(1)}, u32[]{:S(2)}, u32[]{:S(2)}) collective-permute-start(bf16[64,384]{1,0:T(8,128)(2,1)S(1)} %broadcast_select_fusion.26), channel_id=1, source_target_pairs={{0,16},{4,20},{8,24},{12,28},{16,0},{20,4},{24,8},{28,12},{1,17},{... | collective-permute-start | bytes 147464 | tf_op jit(solution)/shard_map/ppermute | solution.py:497
  204.3 22.2 %collective-permute-start.34 = (bf16[640,512]{1,0:T(8,128)(2,1)S(1)}, bf16[640,512]{1,0:T(8,128)(2,1)S(1)}, u32[]{:S(2)}, u32[]{:S(2)}) collective-permute-start(bf16[640,512]{1,0:T(8,128)(2,1)S(1)} %add_convert_fusion.1), channel_id=1, source_target_pairs={{0,2},{1,3},{2,0},{3,1},{4,6},{5,7},{6,4},{7,5},{8,10},{9,11},{10,... | collective-permute-start | bytes 1966088 | tf_op jit(solution)/shard_map/ppermute | solution.py:491
  206.0 8.9 %collective-permute-start.29 = (bf16[64,384]{1,0:T(8,128)(2,1)S(1)}, bf16[64,384]{1,0:T(8,128)(2,1)S(1)}, u32[]{:S(2)}, u32[]{:S(2)}) collective-permute-start(bf16[64,384]{1,0:T(8,128)(2,1)S(1)} %add_convert_fusion.14), channel_id=1, source_target_pairs={{0,16},{4,20},{8,24},{12,28},{16,0},{20,4},{24,8},{28,12},{1,17},{... | collective-permute-start | bytes 147464 | tf_op jit(solution)/shard_map/ppermute | solution.py:497
  215.0 4.7 %collective-permute-start.30 = (bf16[128,384]{1,0:T(8,128)(2,1)S(1)}, bf16[128,384]{1,0:T(8,128)(2,1)S(1)}, u32[]{:S(2)}, u32[]{:S(2)}) collective-permute-start(bf16[128,384]{1,0:T(8,128)(2,1)S(1)} %pad_maximum_fusion.12), channel_id=1, source_target_pairs={{0,8},{4,12},{8,0},{12,4},{16,24},{20,28},{24,16},{28,20},{1,9},{5... | collective-permute-start | bytes 294920 | tf_op jit(solution)/shard_map/ppermute | solution.py:497
  216.7 11.3 %collective-permute-start.44 = (bf16[256,512]{1,0:T(8,128)(2,1)S(1)}, bf16[256,512]{1,0:T(8,128)(2,1)S(1)}, u32[]{:S(2)}, u32[]{:S(2)}) collective-permute-start(bf16[256,512]{1,0:T(8,128)(2,1)S(1)} %broadcast_select_fusion.5), channel_id=1, source_target_pairs={{0,4},{4,0},{8,12},{12,8},{16,20},{20,16},{24,28},{28,24},{1,5},{5... | collective-permute-start | bytes 786440 | tf_op jit(solution)/shard_map/ppermute | solution.py:497
  219.8 19.0 %collective-permute-start.31 = (bf16[256,384]{1,0:T(8,128)(2,1)S(1)}, bf16[256,384]{1,0:T(8,128)(2,1)S(1)}, u32[]{:S(2)}, u32[]{:S(2)}) collective-permute-start(bf16[256,384]{1,0:T(8,128)(2,1)S(1)} %pad_maximum_fusion.9), channel_id=1, source_target_pairs={{0,4},{4,0},{8,12},{12,8},{16,20},{20,16},{24,28},{28,24},{1,5},{5... | collective-permute-start | bytes 589832 | tf_op jit(solution)/shard_map/ppermute | solution.py:497
  227.9 23.5 %collective-permute-start.35 = (bf16[320,512]{1,0:T(8,128)(2,1)S(1)}, bf16[320,512]{1,0:T(8,128)(2,1)S(1)}, u32[]{:S(2)}, u32[]{:S(2)}) collective-permute-start(bf16[320,512]{1,0:T(8,128)(2,1)S(1)} %broadcast_select_fusion.2), channel_id=1, source_target_pairs={{0,4},{4,0},{8,12},{12,8},{16,20},{20,16},{24,28},{28,24},{1,5},{5... | collective-permute-start | bytes 983048 | tf_op jit(solution)/shard_map/ppermute | solution.py:497
  228.2 18.9 %collective-permute-start.45 = (bf16[128,512]{1,0:T(8,128)(2,1)S(1)}, bf16[128,512]{1,0:T(8,128)(2,1)S(1)}, u32[]{:S(2)}, u32[]{:S(2)}) collective-permute-start(bf16[128,512]{1,0:T(8,128)(2,1)S(1)} %broadcast_select_fusion.14), channel_id=1, source_target_pairs={{0,8},{4,12},{8,0},{12,4},{16,24},{20,28},{24,16},{28,20},{1,9},{5... | collective-permute-start | bytes 393224 | tf_op jit(solution)/shard_map/ppermute | solution.py:497
  232.7 3.9 %collective-permute-start.21 = (f32[52,128]{1,0:T(8,128)S(1)}, f32[52,128]{1,0:T(8,128)S(1)}, u32[]{:S(2)}, u32[]{:S(2)}) collective-permute-start(f32[52,128]{1,0:T(8,128)S(1)} %fusion.32), channel_id=1, source_target_pairs={{0,2},{1,3},{2,0},{3,1},{4,6},{5,7},{6,4},{7,5},{8,10},{9,11},{10,... | collective-permute-start | bytes 79880 | tf_op jit(solution)/shard_map/ppermute | solution.py:647
  236.7 3.9 %collective-permute-start.22 = (f32[52,128]{1,0:T(8,128)S(1)}, f32[52,128]{1,0:T(8,128)S(1)}, u32[]{:S(2)}, u32[]{:S(2)}) collective-permute-start(f32[52,128]{1,0:T(8,128)S(1)} %fusion.54), channel_id=1, source_target_pairs={{0,4},{4,0},{8,12},{12,8},{16,20},{20,16},{24,28},{28,24},{1,5},{5... | collective-permute-start | bytes 79880 | tf_op jit(solution)/shard_map/ppermute | solution.py:497
  240.6 3.9 %collective-permute-start.23 = (f32[52,128]{1,0:T(8,128)S(1)}, f32[52,128]{1,0:T(8,128)S(1)}, u32[]{:S(2)}, u32[]{:S(2)}) collective-permute-start(f32[52,128]{1,0:T(8,128)S(1)} %add.304), channel_id=1, source_target_pairs={{0,8},{4,12},{8,0},{12,4},{16,24},{20,28},{24,16},{28,20},{1,9},{5... | collective-permute-start | bytes 79880 | tf_op jit(solution)/shard_map/ppermute | solution.py:497
  244.5 5.1 %collective-permute-start.24 = (f32[52,128]{1,0:T(8,128)S(1)}, f32[52,128]{1,0:T(8,128)S(1)}, u32[]{:S(2)}, u32[]{:S(2)}) collective-permute-start(f32[52,128]{1,0:T(8,128)S(1)} %add.305), channel_id=1, source_target_pairs={{0,16},{4,20},{8,24},{12,28},{16,0},{20,4},{24,8},{28,12},{1,17},{... | collective-permute-start | bytes 79880 | tf_op jit(solution)/shard_map/ppermute | solution.py:497
  247.2 6.1 %collective-permute-start.46 = (bf16[64,512]{1,0:T(8,128)(2,1)S(1)}, bf16[64,512]{1,0:T(8,128)(2,1)S(1)}, u32[]{:S(2)}, u32[]{:S(2)}) collective-permute-start(bf16[64,512]{1,0:T(8,128)(2,1)S(1)} %broadcast_select_fusion.23), channel_id=1, source_target_pairs={{0,16},{4,20},{8,24},{12,28},{16,0},{20,4},{24,8},{28,12},{1,17},{... | collective-permute-start | bytes 196616 | tf_op jit(solution)/shard_map/ppermute | solution.py:497
  251.6 6.3 %collective-permute-start.36 = (bf16[160,512]{1,0:T(8,128)(2,1)S(1)}, bf16[160,512]{1,0:T(8,128)(2,1)S(1)}, u32[]{:S(2)}, u32[]{:S(2)}) collective-permute-start(bf16[160,512]{1,0:T(8,128)(2,1)S(1)} %broadcast_select_fusion.11), channel_id=1, source_target_pairs={{0,8},{4,12},{8,0},{12,4},{16,24},{20,28},{24,16},{28,20},{1,9},{5... | collective-permute-start | bytes 491528 | tf_op jit(solution)/shard_map/ppermute | solution.py:497
  253.3 6.7 %collective-permute-start.47 = (bf16[64,512]{1,0:T(8,128)(2,1)S(1)}, bf16[64,512]{1,0:T(8,128)(2,1)S(1)}, u32[]{:S(2)}, u32[]{:S(2)}) collective-permute-start(bf16[64,512]{1,0:T(8,128)(2,1)S(1)} %add_convert_fusion.13), channel_id=1, source_target_pairs={{0,16},{4,20},{8,24},{12,28},{16,0},{20,4},{24,8},{28,12},{1,17},{... | collective-permute-start | bytes 196616 | tf_op jit(solution)/shard_map/ppermute | solution.py:497
  258.0 6.6 %collective-permute-start.37 = (bf16[80,512]{1,0:T(8,128)(2,1)S(1)}, bf16[80,512]{1,0:T(8,128)(2,1)S(1)}, u32[]{:S(2)}, u32[]{:S(2)}) collective-permute-start(bf16[80,512]{1,0:T(8,128)(2,1)S(1)} %broadcast_select_fusion.20), channel_id=1, source_target_pairs={{0,16},{4,20},{8,24},{12,28},{16,0},{20,4},{24,8},{28,12},{1,17},{... | collective-permute-start | bytes 245768 | tf_op jit(solution)/shard_map/ppermute | solution.py:497
  264.6 6.1 %collective-permute-start.38 = (bf16[80,512]{1,0:T(8,128)(2,1)S(1)}, bf16[80,512]{1,0:T(8,128)(2,1)S(1)}, u32[]{:S(2)}, u32[]{:S(2)}) collective-permute-start(bf16[80,512]{1,0:T(8,128)(2,1)S(1)} %add_convert_fusion.12), channel_id=1, source_target_pairs={{0,16},{4,20},{8,24},{12,28},{16,0},{20,4},{24,8},{28,12},{1,17},{... | collective-permute-start | bytes 245768 | tf_op jit(solution)/shard_map/ppermute | solution.py:497
  265.5 5.9 %collective-permute-start.48 = (bf16[128,512]{1,0:T(8,128)(2,1)S(1)}, bf16[128,512]{1,0:T(8,128)(2,1)S(1)}, u32[]{:S(2)}, u32[]{:S(2)}) collective-permute-start(bf16[128,512]{1,0:T(8,128)(2,1)S(1)} %pad_maximum_fusion.11), channel_id=1, source_target_pairs={{0,8},{4,12},{8,0},{12,4},{16,24},{20,28},{24,16},{28,20},{1,9},{5... | collective-permute-start | bytes 393224 | tf_op jit(solution)/shard_map/ppermute | solution.py:497
  270.7 5.4 %collective-permute-start.39 = (bf16[160,512]{1,0:T(8,128)(2,1)S(1)}, bf16[160,512]{1,0:T(8,128)(2,1)S(1)}, u32[]{:S(2)}, u32[]{:S(2)}) collective-permute-start(bf16[160,512]{1,0:T(8,128)(2,1)S(1)} %pad_maximum_fusion.10), channel_id=1, source_target_pairs={{0,8},{4,12},{8,0},{12,4},{16,24},{20,28},{24,16},{28,20},{1,9},{5... | collective-permute-start | bytes 491528 | tf_op jit(solution)/shard_map/ppermute | solution.py:497
  271.5 6.4 %collective-permute-start.49 = (bf16[256,512]{1,0:T(8,128)(2,1)S(1)}, bf16[256,512]{1,0:T(8,128)(2,1)S(1)}, u32[]{:S(2)}, u32[]{:S(2)}) collective-permute-start(bf16[256,512]{1,0:T(8,128)(2,1)S(1)} %pad_maximum_fusion.8), channel_id=1, source_target_pairs={{0,4},{4,0},{8,12},{12,8},{16,20},{20,16},{24,28},{28,24},{1,5},{5... | collective-permute-start | bytes 786440 | tf_op jit(solution)/shard_map/ppermute | solution.py:497
  276.1 7.1 %collective-permute-start.40 = (bf16[320,512]{1,0:T(8,128)(2,1)S(1)}, bf16[320,512]{1,0:T(8,128)(2,1)S(1)}, u32[]{:S(2)}, u32[]{:S(2)}) collective-permute-start(bf16[320,512]{1,0:T(8,128)(2,1)S(1)} %pad_maximum_fusion.7), channel_id=1, source_target_pairs={{0,4},{4,0},{8,12},{12,8},{16,20},{20,16},{24,28},{28,24},{1,5},{5... | collective-permute-start | bytes 983048 | tf_op jit(solution)/shard_map/ppermute | solution.py:497
  (34 other events, 201.7 us)
